TPU v7x, 128 devices: a whole 4x4x4 slice. The times are simulated.
128 devices in a mesh: section: 8 (over y, core), tok: 16 (over x, z).
Axes of the slice: x: 4, y: 4, z: 4, core: 2. Of those that a mesh axis runs over, the one named last changes fastest.
Arguments:
- coords: float32 [8, 3, 3456], P('section', None, 'tok'), may hold values from -6 to 6
- atom_single: bfloat16 [3456, 128], P('tok'), may hold values from -6 to 6
- token_atoms: int32 [384], P('tok'), may hold values from 1 to 24, as said below
- cond_single: bfloat16 [384, 768], P('tok'), may hold values from -6 to 6
- pair_bias: bfloat16 [8, 16, 384, 384], P('section', None, 'tok'), may hold values from -4 to 330
- w_coord: float32 [3, 128], replicated, may hold values from -4 to 4
- w_in: bfloat16 [128, 768], replicated, may hold values from -1.5 to 1.5
- w_ada: bfloat16 [8, 768, 3072], P('section'), may hold values from -0.21875 to 0.21875
- w_qkv: bfloat16 [8, 768, 2304], P('section'), may hold values from -0.21875 to 0.21875
- w_out: bfloat16 [8, 768, 768], P('section'), may hold values from -0.21875 to 0.21875
- w_ff: bfloat16 [8, 768, 3072], P('section'), may hold values from -0.21875 to 0.21875
- w_down: bfloat16 [8, 1536, 768], P('section'), may hold values from -0.15625 to 0.15625
Outputs:
- token_out: bfloat16 [8, 384, 768], P('section', 'tok')
Inputs may be any that keep to these rules, and one draw needn't show every extreme that they name: `token_atoms`: the first 192 tokens each have 10 to 24 atoms; the later tokens are single-atom ligand tokens.
All inputs are finite; a program needn't handle non-finite values.
Results may differ from a plain program's by a relative error of at most 0.02.
Values may be sent and summed in bfloat16 or wider, within the bound.
A program may use at most 64 MiB of HBM per device.

v0:
```python
import jax
import jax.numpy as jnp
from jax import lax
from jax.sharding import PartitionSpec as P

HEADS = 16
HEAD_DIM = 48
FF = 1536


def passed_along(x, axis, by):
    devices = lax.axis_size(axis)
    pairs = [(i, i + by) for i in range(devices) if 0 <= i + by < devices]
    return lax.ppermute(x, axis, pairs)


def layer_norm(values):
    centre = values - jnp.mean(values, axis=-1, keepdims=True)
    return centre * lax.rsqrt(jnp.mean(centre * centre, axis=-1, keepdims=True) + 1e-05)


def body(
    coords,
    atom_single,
    token_atoms,
    cond_single,
    pair_bias,
    w_coord,
    w_in,
    w_ada,
    w_qkv,
    w_out,
    w_ff,
    w_down,
):
    section_count = lax.axis_size("section")
    section_index = lax.axis_index("section")
    tok_index = lax.axis_index("tok")
    tok_dev = cond_single.shape[0]
    atom_dev = atom_single.shape[0]
    width = cond_single.shape[1]
    counts_all = lax.all_gather(token_atoms, "tok", axis=0, tiled=True)
    starts = jnp.cumsum(counts_all) - counts_all
    atom_place = tok_index * atom_dev + jnp.arange(atom_dev, dtype=jnp.int32)
    atom_token = jnp.sum((starts[None, :] <= atom_place[:, None]).astype(jnp.int32), axis=1) - 1
    points = coords[0]
    atom_act = (
        atom_single.astype(jnp.float32)
        + points[0][:, None] * w_coord[0][None, :]
        + points[1][:, None] * w_coord[1][None, :]
        + points[2][:, None] * w_coord[2][None, :]
    )
    atom_act = jax.nn.relu(atom_act).astype(jnp.bfloat16)
    token_rows = jnp.arange(tok_dev * lax.axis_size("tok"), dtype=jnp.int32)
    membership = (atom_token[None, :] == token_rows[:, None]).astype(jnp.bfloat16)
    pooled = lax.psum_scatter(
        jnp.dot(membership, atom_act, preferred_element_type=jnp.float32),
        "tok",
        scatter_dimension=0,
        tiled=True,
    )
    averaged = (pooled / token_atoms.astype(jnp.float32)[:, None]).astype(jnp.bfloat16)
    entering_state = jnp.dot(averaged, w_in, preferred_element_type=jnp.float32)
    inputs = lax.all_gather(entering_state[None], "section", axis=0, tiled=True)
    poses = inputs.shape[0]
    conditioning = jnp.dot(cond_single, w_ada[0], preferred_element_type=jnp.float32)
    scale_attn = conditioning[:, :width]
    shift_attn = conditioning[:, width : 2 * width]
    scale_trans = conditioning[:, 2 * width : 3 * width]
    shift_trans = conditioning[:, 3 * width :]
    weight_qkv = w_qkv[0]
    weight_out = w_out[0]
    weight_ff = w_ff[0]
    weight_down = w_down[0]
    bias_rows = pair_bias[0].astype(jnp.float32)

    def token_layer(state):
        normed = (layer_norm(state) * jax.nn.sigmoid(scale_attn) + shift_attn).astype(jnp.bfloat16)
        projected = jnp.dot(normed, weight_qkv, preferred_element_type=jnp.float32).astype(
            jnp.bfloat16
        )
        queries = projected[:, :width]
        keys_all, values_all = (
            lax.all_gather(projected[:, width : 2 * width], "tok", axis=0, tiled=True),
            lax.all_gather(projected[:, 2 * width :], "tok", axis=0, tiled=True),
        )
        query_heads = queries.reshape(tok_dev, HEADS, HEAD_DIM)
        key_heads = keys_all.reshape(-1, HEADS, HEAD_DIM)
        value_heads = values_all.reshape(-1, HEADS, HEAD_DIM)
        scores = (
            jnp.einsum("ihd,jhd->hij", query_heads, key_heads, preferred_element_type=jnp.float32)
            * HEAD_DIM ** (-0.5)
            + bias_rows
        )
        probs = jax.nn.softmax(scores, axis=-1).astype(jnp.bfloat16)
        attended = jnp.einsum(
            "hij,jhd->ihd", probs, value_heads, preferred_element_type=jnp.float32
        )
        attended = attended.reshape(tok_dev, width).astype(jnp.bfloat16)
        state = state + jnp.dot(attended, weight_out, preferred_element_type=jnp.float32)
        normed_t = (layer_norm(state) * jax.nn.sigmoid(scale_trans) + shift_trans).astype(
            jnp.bfloat16
        )
        gate_up = jnp.dot(normed_t, weight_ff, preferred_element_type=jnp.float32)
        hidden = (jax.nn.silu(gate_up[:, :FF]) * gate_up[:, FF:]).astype(jnp.bfloat16)
        return state + jnp.dot(hidden, weight_down, preferred_element_type=jnp.float32)

    def tick(tick_count, carry):
        current, finished = carry
        incoming = lax.dynamic_index_in_dim(
            inputs, jnp.minimum(tick_count, poses - 1), 0, keepdims=False
        )
        entering = jnp.where(section_index == 0, incoming, current)
        result = token_layer(entering)
        pose_index = tick_count - section_index
        storing = (section_index == section_count - 1) & (pose_index >= 0) & (pose_index < poses)
        slot_index = jnp.clip(pose_index, 0, poses - 1)
        finished_rows = layer_norm(result).astype(jnp.bfloat16)
        previous = lax.dynamic_index_in_dim(finished, slot_index, 0, keepdims=False)
        finished = lax.dynamic_update_index_in_dim(
            finished, jnp.where(storing, finished_rows, previous), slot_index, 0
        )
        current = passed_along(result, "section", 1)
        return (current, finished)

    start_state = jnp.zeros((tok_dev, width), jnp.float32)
    start_finished = jnp.zeros((poses, tok_dev, width), jnp.bfloat16)
    _, finished = lax.fori_loop(0, poses + section_count - 1, tick, (start_state, start_finished))
    received = lax.all_to_all(finished, "section", split_axis=0, concat_axis=0, tiled=True)
    return received[section_count - 1 : section_count]


def solution(mesh):
    return jax.shard_map(
        body,
        mesh=mesh,
        in_specs=(
            P("section", None, "tok"),
            P("tok", None),
            P("tok"),
            P("tok", None),
            P("section", None, "tok", None),
            P(),
            P(),
            P("section", None, None),
            P("section", None, None),
            P("section", None, None),
            P("section", None, None),
            P("section", None, None),
        ),
        out_specs=P("section", "tok", None),
        check_vma=False,
    )
```

profile of v0, /device:TPU:17, one launch (start us, length us, event | category | flops | bytes accessed | tf_op | source)
XLA Modules:
  0.0 1102.7 jit_solution(8336408172021545927)
XLA Ops:
  9.4 13.7 %all-reduce = s32[384]{0:T(512)S(1)} all-reduce(s32[384]{0:T(512)S(1)} %dynamic-update-slice), channel_id=1, replica_groups=mesh['section'=8,'tok'=16] {'tok'}, use_global_device_ids=true, to_apply=%add | all-reduce | flops 384 | bytes 3072
  31.7 65.6 %reduce-scatter.4.cloned.1.call-done = f32[24,128]{1,0:T(8,128)} async-done(((f32[384,128]{1,0:T(8,128)}), f32[24,128]{1,0:T(8,128)}) %reduce-scatter.4.cloned.1.call-update) | async-done | bytes 12304
  98.2 15.5 %all-gather = f32[192,768]{1,0:T(8,128)} all-gather(f32[24,768]{1,0:T(8,128)S(1)} %fusion.37), channel_id=2, replica_groups=mesh['section'=8,'tok'=16] {'section'}, dimensions={0}, use_global_device_ids=true | all-gather | bytes 663552 | tf_op jit(solution)/shard_map/all_gather | solution.py:64
  114.4 970.3 %while.17 = (s32[]{:T(128)}, f32[24,768]{1,0:T(8,128)S(1)}, bf16[8,24,768]{2,1,0:T(8,128)(2,1)}, pred[]{:T(512)}, f32[8,24,768]{2,1,0:T(8,128)}, /*index=5*/f32[...) while((s32[]{:T(128)}, f32[24,768]{1,0:T(8,128)S(1)}, ...), condition=%wide.region_13.14_spmd, body=%wide.region_4.13_spmd.sunk | while | flops 313363648 | bytes 32225252 | solution.py:128
  118.4 18.9 %all_gather.29 = bf16[384,768]{1,0:T(8,128)(2,1)S(1)} all-gather(bf16[24,768]{1,0:T(8,128)(2,1)S(1)} %get-tuple-element.498), channel_id=1, replica_groups=mesh['section'=8,'tok'=16] {'tok'}, dimensions={0}, use_global_device_ids=true | all-gather | bytes 626688 | tf_op jit(solution)/shard_map/while/body/eval_jaxpr/all_gather | solution.py:84
  138.2 16.4 %all_gather.28 = bf16[384,768]{1,0:T(8,128)(2,1)S(1)} all-gather(bf16[24,768]{1,0:T(8,128)(2,1)S(1)} %get-tuple-element.497), channel_id=1, replica_groups=mesh['section'=8,'tok'=16] {'tok'}, dimensions={0}, use_global_device_ids=true | all-gather | bytes 626688 | tf_op jit(solution)/shard_map/while/body/eval_jaxpr/all_gather | solution.py:85
  159.5 3.1 fusion.93
  163.2 14.5 %collective-permute-start = (f32[24,768]{1,0:T(8,128)S(1)}, f32[24,768]{1,0:T(8,128)S(1)}, u32[]{:S(2)}, u32[]{:S(2)}) collective-permute-start(f32[24,768]{1,0:T(8,128)S(1)} %get-tuple-element.502), channel_id=1, source_target_pairs={{0,16},{16,32},{32,48},{48,64},{64,80},{80,96},{96,112},{1,17},{17... | collective-permute-start | bytes 221192 | tf_op jit(solution)/shard_map/while/body/eval_jaxpr/ppermute | solution.py:14
  183.4 18.2 %all_gather.29 = bf16[384,768]{1,0:T(8,128)(2,1)S(1)} all-gather(bf16[24,768]{1,0:T(8,128)(2,1)S(1)} %get-tuple-element.498), channel_id=1, replica_groups=mesh['section'=8,'tok'=16] {'tok'}, dimensions={0}, use_global_device_ids=true | all-gather | bytes 626688 | tf_op jit(solution)/shard_map/while/body/eval_jaxpr/all_gather | solution.py:84
  202.6 17.1 %all_gather.28 = bf16[384,768]{1,0:T(8,128)(2,1)S(1)} all-gather(bf16[24,768]{1,0:T(8,128)(2,1)S(1)} %get-tuple-element.497), channel_id=1, replica_groups=mesh['section'=8,'tok'=16] {'tok'}, dimensions={0}, use_global_device_ids=true | all-gather | bytes 626688 | tf_op jit(solution)/shard_map/while/body/eval_jaxpr/all_gather | solution.py:85
  224.6 3.1 fusion.93
  228.3 14.1 %collective-permute-start = (f32[24,768]{1,0:T(8,128)S(1)}, f32[24,768]{1,0:T(8,128)S(1)}, u32[]{:S(2)}, u32[]{:S(2)}) collective-permute-start(f32[24,768]{1,0:T(8,128)S(1)} %get-tuple-element.502), channel_id=1, source_target_pairs={{0,16},{16,32},{32,48},{48,64},{64,80},{80,96},{96,112},{1,17},{17... | collective-permute-start | bytes 221192 | tf_op jit(solution)/shard_map/while/body/eval_jaxpr/ppermute | solution.py:14
  248.0 18.2 %all_gather.29 = bf16[384,768]{1,0:T(8,128)(2,1)S(1)} all-gather(bf16[24,768]{1,0:T(8,128)(2,1)S(1)} %get-tuple-element.498), channel_id=1, replica_groups=mesh['section'=8,'tok'=16] {'tok'}, dimensions={0}, use_global_device_ids=true | all-gather | bytes 626688 | tf_op jit(solution)/shard_map/while/body/eval_jaxpr/all_gather | solution.py:84
  267.1 17.2 %all_gather.28 = bf16[384,768]{1,0:T(8,128)(2,1)S(1)} all-gather(bf16[24,768]{1,0:T(8,128)(2,1)S(1)} %get-tuple-element.497), channel_id=1, replica_groups=mesh['section'=8,'tok'=16] {'tok'}, dimensions={0}, use_global_device_ids=true | all-gather | bytes 626688 | tf_op jit(solution)/shard_map/while/body/eval_jaxpr/all_gather | solution.py:85
  289.1 3.1 fusion.93
  292.9 14.0 %collective-permute-start = (f32[24,768]{1,0:T(8,128)S(1)}, f32[24,768]{1,0:T(8,128)S(1)}, u32[]{:S(2)}, u32[]{:S(2)}) collective-permute-start(f32[24,768]{1,0:T(8,128)S(1)} %get-tuple-element.502), channel_id=1, source_target_pairs={{0,16},{16,32},{32,48},{48,64},{64,80},{80,96},{96,112},{1,17},{17... | collective-permute-start | bytes 221192 | tf_op jit(solution)/shard_map/while/body/eval_jaxpr/ppermute | solution.py:14
  312.5 18.3 %all_gather.29 = bf16[384,768]{1,0:T(8,128)(2,1)S(1)} all-gather(bf16[24,768]{1,0:T(8,128)(2,1)S(1)} %get-tuple-element.498), channel_id=1, replica_groups=mesh['section'=8,'tok'=16] {'tok'}, dimensions={0}, use_global_device_ids=true | all-gather | bytes 626688 | tf_op jit(solution)/shard_map/while/body/eval_jaxpr/all_gather | solution.py:84
  331.8 17.1 %all_gather.28 = bf16[384,768]{1,0:T(8,128)(2,1)S(1)} all-gather(bf16[24,768]{1,0:T(8,128)(2,1)S(1)} %get-tuple-element.497), channel_id=1, replica_groups=mesh['section'=8,'tok'=16] {'tok'}, dimensions={0}, use_global_device_ids=true | all-gather | bytes 626688 | tf_op jit(solution)/shard_map/while/body/eval_jaxpr/all_gather | solution.py:85
  353.7 3.1 fusion.93
  357.4 13.9 %collective-permute-start = (f32[24,768]{1,0:T(8,128)S(1)}, f32[24,768]{1,0:T(8,128)S(1)}, u32[]{:S(2)}, u32[]{:S(2)}) collective-permute-start(f32[24,768]{1,0:T(8,128)S(1)} %get-tuple-element.502), channel_id=1, source_target_pairs={{0,16},{16,32},{32,48},{48,64},{64,80},{80,96},{96,112},{1,17},{17... | collective-permute-start | bytes 221192 | tf_op jit(solution)/shard_map/while/body/eval_jaxpr/ppermute | solution.py:14
  377.0 18.4 %all_gather.29 = bf16[384,768]{1,0:T(8,128)(2,1)S(1)} all-gather(bf16[24,768]{1,0:T(8,128)(2,1)S(1)} %get-tuple-element.498), channel_id=1, replica_groups=mesh['section'=8,'tok'=16] {'tok'}, dimensions={0}, use_global_device_ids=true | all-gather | bytes 626688 | tf_op jit(solution)/shard_map/while/body/eval_jaxpr/all_gather | solution.py:84
  396.4 16.4 %all_gather.28 = bf16[384,768]{1,0:T(8,128)(2,1)S(1)} all-gather(bf16[24,768]{1,0:T(8,128)(2,1)S(1)} %get-tuple-element.497), channel_id=1, replica_groups=mesh['section'=8,'tok'=16] {'tok'}, dimensions={0}, use_global_device_ids=true | all-gather | bytes 626688 | tf_op jit(solution)/shard_map/while/body/eval_jaxpr/all_gather | solution.py:85
  417.7 3.1 fusion.93
  421.4 14.5 %collective-permute-start = (f32[24,768]{1,0:T(8,128)S(1)}, f32[24,768]{1,0:T(8,128)S(1)}, u32[]{:S(2)}, u32[]{:S(2)}) collective-permute-start(f32[24,768]{1,0:T(8,128)S(1)} %get-tuple-element.502), channel_id=1, source_target_pairs={{0,16},{16,32},{32,48},{48,64},{64,80},{80,96},{96,112},{1,17},{17... | collective-permute-start | bytes 221192 | tf_op jit(solution)/shard_map/while/body/eval_jaxpr/ppermute | solution.py:14
  441.6 18.6 %all_gather.29 = bf16[384,768]{1,0:T(8,128)(2,1)S(1)} all-gather(bf16[24,768]{1,0:T(8,128)(2,1)S(1)} %get-tuple-element.498), channel_id=1, replica_groups=mesh['section'=8,'tok'=16] {'tok'}, dimensions={0}, use_global_device_ids=true | all-gather | bytes 626688 | tf_op jit(solution)/shard_map/while/body/eval_jaxpr/all_gather | solution.py:84
  461.2 16.2 %all_gather.28 = bf16[384,768]{1,0:T(8,128)(2,1)S(1)} all-gather(bf16[24,768]{1,0:T(8,128)(2,1)S(1)} %get-tuple-element.497), channel_id=1, replica_groups=mesh['section'=8,'tok'=16] {'tok'}, dimensions={0}, use_global_device_ids=true | all-gather | bytes 626688 | tf_op jit(solution)/shard_map/while/body/eval_jaxpr/all_gather | solution.py:85
  482.3 3.1 fusion.93
  486.0 14.4 %collective-permute-start = (f32[24,768]{1,0:T(8,128)S(1)}, f32[24,768]{1,0:T(8,128)S(1)}, u32[]{:S(2)}, u32[]{:S(2)}) collective-permute-start(f32[24,768]{1,0:T(8,128)S(1)} %get-tuple-element.502), channel_id=1, source_target_pairs={{0,16},{16,32},{32,48},{48,64},{64,80},{80,96},{96,112},{1,17},{17... | collective-permute-start | bytes 221192 | tf_op jit(solution)/shard_map/while/body/eval_jaxpr/ppermute | solution.py:14
  506.1 18.8 %all_gather.29 = bf16[384,768]{1,0:T(8,128)(2,1)S(1)} all-gather(bf16[24,768]{1,0:T(8,128)(2,1)S(1)} %get-tuple-element.498), channel_id=1, replica_groups=mesh['section'=8,'tok'=16] {'tok'}, dimensions={0}, use_global_device_ids=true | all-gather | bytes 626688 | tf_op jit(solution)/shard_map/while/body/eval_jaxpr/all_gather | solution.py:84
  525.9 16.2 %all_gather.28 = bf16[384,768]{1,0:T(8,128)(2,1)S(1)} all-gather(bf16[24,768]{1,0:T(8,128)(2,1)S(1)} %get-tuple-element.497), channel_id=1, replica_groups=mesh['section'=8,'tok'=16] {'tok'}, dimensions={0}, use_global_device_ids=true | all-gather | bytes 626688 | tf_op jit(solution)/shard_map/while/body/eval_jaxpr/all_gather | solution.py:85
  547.0 3.1 fusion.93
  550.7 14.5 %collective-permute-start = (f32[24,768]{1,0:T(8,128)S(1)}, f32[24,768]{1,0:T(8,128)S(1)}, u32[]{:S(2)}, u32[]{:S(2)}) collective-permute-start(f32[24,768]{1,0:T(8,128)S(1)} %get-tuple-element.502), channel_id=1, source_target_pairs={{0,16},{16,32},{32,48},{48,64},{64,80},{80,96},{96,112},{1,17},{17... | collective-permute-start | bytes 221192 | tf_op jit(solution)/shard_map/while/body/eval_jaxpr/ppermute | solution.py:14
  570.9 19.7 %all_gather.29 = bf16[384,768]{1,0:T(8,128)(2,1)S(1)} all-gather(bf16[24,768]{1,0:T(8,128)(2,1)S(1)} %get-tuple-element.498), channel_id=1, replica_groups=mesh['section'=8,'tok'=16] {'tok'}, dimensions={0}, use_global_device_ids=true | all-gather | bytes 626688 | tf_op jit(solution)/shard_map/while/body/eval_jaxpr/all_gather | solution.py:84
  591.6 16.0 %all_gather.28 = bf16[384,768]{1,0:T(8,128)(2,1)S(1)} all-gather(bf16[24,768]{1,0:T(8,128)(2,1)S(1)} %get-tuple-element.497), channel_id=1, replica_groups=mesh['section'=8,'tok'=16] {'tok'}, dimensions={0}, use_global_device_ids=true | all-gather | bytes 626688 | tf_op jit(solution)/shard_map/while/body/eval_jaxpr/all_gather | solution.py:85
  612.4 3.1 fusion.93
  616.2 13.8 %collective-permute-start = (f32[24,768]{1,0:T(8,128)S(1)}, f32[24,768]{1,0:T(8,128)S(1)}, u32[]{:S(2)}, u32[]{:S(2)}) collective-permute-start(f32[24,768]{1,0:T(8,128)S(1)} %get-tuple-element.502), channel_id=1, source_target_pairs={{0,16},{16,32},{32,48},{48,64},{64,80},{80,96},{96,112},{1,17},{17... | collective-permute-start | bytes 221192 | tf_op jit(solution)/shard_map/while/body/eval_jaxpr/ppermute | solution.py:14
  635.6 19.6 %all_gather.29 = bf16[384,768]{1,0:T(8,128)(2,1)S(1)} all-gather(bf16[24,768]{1,0:T(8,128)(2,1)S(1)} %get-tuple-element.498), channel_id=1, replica_groups=mesh['section'=8,'tok'=16] {'tok'}, dimensions={0}, use_global_device_ids=true | all-gather | bytes 626688 | tf_op jit(solution)/shard_map/while/body/eval_jaxpr/all_gather | solution.py:84
  656.2 16.1 %all_gather.28 = bf16[384,768]{1,0:T(8,128)(2,1)S(1)} all-gather(bf16[24,768]{1,0:T(8,128)(2,1)S(1)} %get-tuple-element.497), channel_id=1, replica_groups=mesh['section'=8,'tok'=16] {'tok'}, dimensions={0}, use_global_device_ids=true | all-gather | bytes 626688 | tf_op jit(solution)/shard_map/while/body/eval_jaxpr/all_gather | solution.py:85
  677.2 3.1 fusion.93
  680.9 13.8 %collective-permute-start = (f32[24,768]{1,0:T(8,128)S(1)}, f32[24,768]{1,0:T(8,128)S(1)}, u32[]{:S(2)}, u32[]{:S(2)}) collective-permute-start(f32[24,768]{1,0:T(8,128)S(1)} %get-tuple-element.502), channel_id=1, source_target_pairs={{0,16},{16,32},{32,48},{48,64},{64,80},{80,96},{96,112},{1,17},{17... | collective-permute-start | bytes 221192 | tf_op jit(solution)/shard_map/while/body/eval_jaxpr/ppermute | solution.py:14
  700.3 19.2 %all_gather.29 = bf16[384,768]{1,0:T(8,128)(2,1)S(1)} all-gather(bf16[24,768]{1,0:T(8,128)(2,1)S(1)} %get-tuple-element.498), channel_id=1, replica_groups=mesh['section'=8,'tok'=16] {'tok'}, dimensions={0}, use_global_device_ids=true | all-gather | bytes 626688 | tf_op jit(solution)/shard_map/while/body/eval_jaxpr/all_gather | solution.py:84
  720.5 16.0 %all_gather.28 = bf16[384,768]{1,0:T(8,128)(2,1)S(1)} all-gather(bf16[24,768]{1,0:T(8,128)(2,1)S(1)} %get-tuple-element.497), channel_id=1, replica_groups=mesh['section'=8,'tok'=16] {'tok'}, dimensions={0}, use_global_device_ids=true | all-gather | bytes 626688 | tf_op jit(solution)/shard_map/while/body/eval_jaxpr/all_gather | solution.py:85
  741.3 3.1 fusion.93
  745.0 14.4 %collective-permute-start = (f32[24,768]{1,0:T(8,128)S(1)}, f32[24,768]{1,0:T(8,128)S(1)}, u32[]{:S(2)}, u32[]{:S(2)}) collective-permute-start(f32[24,768]{1,0:T(8,128)S(1)} %get-tuple-element.502), channel_id=1, source_target_pairs={{0,16},{16,32},{32,48},{48,64},{64,80},{80,96},{96,112},{1,17},{17... | collective-permute-start | bytes 221192 | tf_op jit(solution)/shard_map/while/body/eval_jaxpr/ppermute | solution.py:14
  765.1 19.1 %all_gather.29 = bf16[384,768]{1,0:T(8,128)(2,1)S(1)} all-gather(bf16[24,768]{1,0:T(8,128)(2,1)S(1)} %get-tuple-element.498), channel_id=1, replica_groups=mesh['section'=8,'tok'=16] {'tok'}, dimensions={0}, use_global_device_ids=true | all-gather | bytes 626688 | tf_op jit(solution)/shard_map/while/body/eval_jaxpr/all_gather | solution.py:84
  785.1 16.0 %all_gather.28 = bf16[384,768]{1,0:T(8,128)(2,1)S(1)} all-gather(bf16[24,768]{1,0:T(8,128)(2,1)S(1)} %get-tuple-element.497), channel_id=1, replica_groups=mesh['section'=8,'tok'=16] {'tok'}, dimensions={0}, use_global_device_ids=true | all-gather | bytes 626688 | tf_op jit(solution)/shard_map/while/body/eval_jaxpr/all_gather | solution.py:85
  806.0 3.1 fusion.93
  809.7 14.5 %collective-permute-start = (f32[24,768]{1,0:T(8,128)S(1)}, f32[24,768]{1,0:T(8,128)S(1)}, u32[]{:S(2)}, u32[]{:S(2)}) collective-permute-start(f32[24,768]{1,0:T(8,128)S(1)} %get-tuple-element.502), channel_id=1, source_target_pairs={{0,16},{16,32},{32,48},{48,64},{64,80},{80,96},{96,112},{1,17},{17... | collective-permute-start | bytes 221192 | tf_op jit(solution)/shard_map/while/body/eval_jaxpr/ppermute | solution.py:14
  829.8 18.9 %all_gather.29 = bf16[384,768]{1,0:T(8,128)(2,1)S(1)} all-gather(bf16[24,768]{1,0:T(8,128)(2,1)S(1)} %get-tuple-element.498), channel_id=1, replica_groups=mesh['section'=8,'tok'=16] {'tok'}, dimensions={0}, use_global_device_ids=true | all-gather | bytes 626688 | tf_op jit(solution)/shard_map/while/body/eval_jaxpr/all_gather | solution.py:84
  849.6 16.1 %all_gather.28 = bf16[384,768]{1,0:T(8,128)(2,1)S(1)} all-gather(bf16[24,768]{1,0:T(8,128)(2,1)S(1)} %get-tuple-element.497), channel_id=1, replica_groups=mesh['section'=8,'tok'=16] {'tok'}, dimensions={0}, use_global_device_ids=true | all-gather | bytes 626688 | tf_op jit(solution)/shard_map/while/body/eval_jaxpr/all_gather | solution.py:85
  870.6 3.1 fusion.93
  874.3 14.6 %collective-permute-start = (f32[24,768]{1,0:T(8,128)S(1)}, f32[24,768]{1,0:T(8,128)S(1)}, u32[]{:S(2)}, u32[]{:S(2)}) collective-permute-start(f32[24,768]{1,0:T(8,128)S(1)} %get-tuple-element.502), channel_id=1, source_target_pairs={{0,16},{16,32},{32,48},{48,64},{64,80},{80,96},{96,112},{1,17},{17... | collective-permute-start | bytes 221192 | tf_op jit(solution)/shard_map/while/body/eval_jaxpr/ppermute | solution.py:14
  894.5 18.7 %all_gather.29 = bf16[384,768]{1,0:T(8,128)(2,1)S(1)} all-gather(bf16[24,768]{1,0:T(8,128)(2,1)S(1)} %get-tuple-element.498), channel_id=1, replica_groups=mesh['section'=8,'tok'=16] {'tok'}, dimensions={0}, use_global_device_ids=true | all-gather | bytes 626688 | tf_op jit(solution)/shard_map/while/body/eval_jaxpr/all_gather | solution.py:84
  914.2 16.1 %all_gather.28 = bf16[384,768]{1,0:T(8,128)(2,1)S(1)} all-gather(bf16[24,768]{1,0:T(8,128)(2,1)S(1)} %get-tuple-element.497), channel_id=1, replica_groups=mesh['section'=8,'tok'=16] {'tok'}, dimensions={0}, use_global_device_ids=true | all-gather | bytes 626688 | tf_op jit(solution)/shard_map/while/body/eval_jaxpr/all_gather | solution.py:85
  935.2 3.1 fusion.93
  938.9 14.7 %collective-permute-start = (f32[24,768]{1,0:T(8,128)S(1)}, f32[24,768]{1,0:T(8,128)S(1)}, u32[]{:S(2)}, u32[]{:S(2)}) collective-permute-start(f32[24,768]{1,0:T(8,128)S(1)} %get-tuple-element.502), channel_id=1, source_target_pairs={{0,16},{16,32},{32,48},{48,64},{64,80},{80,96},{96,112},{1,17},{17... | collective-permute-start | bytes 221192 | tf_op jit(solution)/shard_map/while/body/eval_jaxpr/ppermute | solution.py:14
  959.2 18.7 %all_gather.29 = bf16[384,768]{1,0:T(8,128)(2,1)S(1)} all-gather(bf16[24,768]{1,0:T(8,128)(2,1)S(1)} %get-tuple-element.498), channel_id=1, replica_groups=mesh['section'=8,'tok'=16] {'tok'}, dimensions={0}, use_global_device_ids=true | all-gather | bytes 626688 | tf_op jit(solution)/shard_map/while/body/eval_jaxpr/all_gather | solution.py:84
  978.9 16.0 %all_gather.28 = bf16[384,768]{1,0:T(8,128)(2,1)S(1)} all-gather(bf16[24,768]{1,0:T(8,128)(2,1)S(1)} %get-tuple-element.497), channel_id=1, replica_groups=mesh['section'=8,'tok'=16] {'tok'}, dimensions={0}, use_global_device_ids=true | all-gather | bytes 626688 | tf_op jit(solution)/shard_map/while/body/eval_jaxpr/all_gather | solution.py:85
  1003.5 14.8 %collective-permute-start = (f32[24,768]{1,0:T(8,128)S(1)}, f32[24,768]{1,0:T(8,128)S(1)}, u32[]{:S(2)}, u32[]{:S(2)}) collective-permute-start(f32[24,768]{1,0:T(8,128)S(1)} %get-tuple-element.502), channel_id=1, source_target_pairs={{0,16},{16,32},{32,48},{48,64},{64,80},{80,96},{96,112},{1,17},{17... | collective-permute-start | bytes 221192 | tf_op jit(solution)/shard_map/while/body/eval_jaxpr/ppermute | solution.py:14
  1024.0 18.8 %all_gather.29 = bf16[384,768]{1,0:T(8,128)(2,1)S(1)} all-gather(bf16[24,768]{1,0:T(8,128)(2,1)S(1)} %get-tuple-element.498), channel_id=1, replica_groups=mesh['section'=8,'tok'=16] {'tok'}, dimensions={0}, use_global_device_ids=true | all-gather | bytes 626688 | tf_op jit(solution)/shard_map/while/body/eval_jaxpr/all_gather | solution.py:84
  1043.8 16.3 %all_gather.28 = bf16[384,768]{1,0:T(8,128)(2,1)S(1)} all-gather(bf16[24,768]{1,0:T(8,128)(2,1)S(1)} %get-tuple-element.497), channel_id=1, replica_groups=mesh['section'=8,'tok'=16] {'tok'}, dimensions={0}, use_global_device_ids=true | all-gather | bytes 626688 | tf_op jit(solution)/shard_map/while/body/eval_jaxpr/all_gather | solution.py:85
  1064.9 3.1 fusion.93
  1068.6 14.5 %collective-permute-start = (f32[24,768]{1,0:T(8,128)S(1)}, f32[24,768]{1,0:T(8,128)S(1)}, u32[]{:S(2)}, u32[]{:S(2)}) collective-permute-start(f32[24,768]{1,0:T(8,128)S(1)} %get-tuple-element.502), channel_id=1, source_target_pairs={{0,16},{16,32},{32,48},{48,64},{64,80},{80,96},{96,112},{1,17},{17... | collective-permute-start | bytes 221192 | tf_op jit(solution)/shard_map/while/body/eval_jaxpr/ppermute | solution.py:14
  1084.7 10.5 all_to_all.5
  (524 shorter events, 194.9 us)
Async XLA Ops:
  6.5 90.8 %copy-start = (bf16[128,768]{1,0:T(8,128)(2,1)S(1)}, bf16[128,768]{1,0:T(8,128)(2,1)}, u32[]{:S(2)}) copy-start(bf16[128,768]{1,0:T(8,128)(2,1)} %param.20) | copy-start | bytes 589828
  6.5 25.2 %copy-start.5 = (bf16[1,16,24,384]{3,2,1,0:T(8,128)(2,1)S(1)}, bf16[1,16,24,384]{3,2,1,0:T(8,128)(2,1)}, u32[]{:S(2)}) copy-start(bf16[1,16,24,384]{3,2,1,0:T(8,128)(2,1)} %param.18) | copy-start | bytes 884740
  6.5 90.8 %reduce-scatter.4.cloned.1.call-start = ((), (), s32[]{:S(2)}) async-start(), calls=%async_computation.2 | async-start | bytes 208896
  114.4 23.6 %copy-start.3 = (f32[24,768]{1,0:T(8,128)}, f32[24,768]{1,0:T(8,128)S(1)}, u32[]{:S(2)}) copy-start(f32[24,768]{1,0:T(8,128)S(1)} %get-tuple-element.550) | copy-start | bytes 221188 | tf_op jit(solution)/shard_map/while
  138.0 21.5 %copy-start.2 = (f32[24,768]{1,0:T(8,128)S(1)}, f32[24,768]{1,0:T(8,128)}, u32[]{:S(2)}) copy-start(f32[24,768]{1,0:T(8,128)} %get-tuple-element.554) | copy-start | bytes 221188 | tf_op jit(solution)/shard_map/while
  156.4 6.3 copy-start.1
  159.5 19.9 %copy-start.4 = (f32[24,768]{1,0:T(8,128)S(1)}, f32[24,768]{1,0:T(8,128)}, u32[]{:S(2)}) copy-start(f32[24,768]{1,0:T(8,128)} %copy-done.3) | copy-start | bytes 221188 | tf_op jit(solution)/shard_map/while
  163.2 16.2 %collective-permute-start = (f32[24,768]{1,0:T(8,128)S(1)}, f32[24,768]{1,0:T(8,128)S(1)}, u32[]{:S(2)}, u32[]{:S(2)}) collective-permute-start(f32[24,768]{1,0:T(8,128)S(1)} %get-tuple-element.502), channel_id=1, source_target_pairs={{0,16},{16,32},{32,48},{48,64},{64,80},{80,96},{96,112},{1,17},{17... | collective-permute-start | bytes 221192 | tf_op jit(solution)/shard_map/while/body/eval_jaxpr/ppermute | solution.py:14
  179.4 22.9 %copy-start.3 = (f32[24,768]{1,0:T(8,128)}, f32[24,768]{1,0:T(8,128)S(1)}, u32[]{:S(2)}) copy-start(f32[24,768]{1,0:T(8,128)S(1)} %get-tuple-element.550) | copy-start | bytes 221188 | tf_op jit(solution)/shard_map/while
  202.3 22.2 %copy-start.2 = (f32[24,768]{1,0:T(8,128)S(1)}, f32[24,768]{1,0:T(8,128)}, u32[]{:S(2)}) copy-start(f32[24,768]{1,0:T(8,128)} %get-tuple-element.554) | copy-start | bytes 221188 | tf_op jit(solution)/shard_map/while
  224.5 19.5 %copy-start.4 = (f32[24,768]{1,0:T(8,128)S(1)}, f32[24,768]{1,0:T(8,128)}, u32[]{:S(2)}) copy-start(f32[24,768]{1,0:T(8,128)} %copy-done.3) | copy-start | bytes 221188 | tf_op jit(solution)/shard_map/while
  228.3 15.7 %collective-permute-start = (f32[24,768]{1,0:T(8,128)S(1)}, f32[24,768]{1,0:T(8,128)S(1)}, u32[]{:S(2)}, u32[]{:S(2)}) collective-permute-start(f32[24,768]{1,0:T(8,128)S(1)} %get-tuple-element.502), channel_id=1, source_target_pairs={{0,16},{16,32},{32,48},{48,64},{64,80},{80,96},{96,112},{1,17},{17... | collective-permute-start | bytes 221192 | tf_op jit(solution)/shard_map/while/body/eval_jaxpr/ppermute | solution.py:14
  244.0 22.9 %copy-start.3 = (f32[24,768]{1,0:T(8,128)}, f32[24,768]{1,0:T(8,128)S(1)}, u32[]{:S(2)}) copy-start(f32[24,768]{1,0:T(8,128)S(1)} %get-tuple-element.550) | copy-start | bytes 221188 | tf_op jit(solution)/shard_map/while
  266.9 22.3 %copy-start.2 = (f32[24,768]{1,0:T(8,128)S(1)}, f32[24,768]{1,0:T(8,128)}, u32[]{:S(2)}) copy-start(f32[24,768]{1,0:T(8,128)} %get-tuple-element.554) | copy-start | bytes 221188 | tf_op jit(solution)/shard_map/while
  289.1 19.4 %copy-start.4 = (f32[24,768]{1,0:T(8,128)S(1)}, f32[24,768]{1,0:T(8,128)}, u32[]{:S(2)}) copy-start(f32[24,768]{1,0:T(8,128)} %copy-done.3) | copy-start | bytes 221188 | tf_op jit(solution)/shard_map/while
  292.9 15.7 %collective-permute-start = (f32[24,768]{1,0:T(8,128)S(1)}, f32[24,768]{1,0:T(8,128)S(1)}, u32[]{:S(2)}, u32[]{:S(2)}) collective-permute-start(f32[24,768]{1,0:T(8,128)S(1)} %get-tuple-element.502), channel_id=1, source_target_pairs={{0,16},{16,32},{32,48},{48,64},{64,80},{80,96},{96,112},{1,17},{17... | collective-permute-start | bytes 221192 | tf_op jit(solution)/shard_map/while/body/eval_jaxpr/ppermute | solution.py:14
  308.5 23.0 %copy-start.3 = (f32[24,768]{1,0:T(8,128)}, f32[24,768]{1,0:T(8,128)S(1)}, u32[]{:S(2)}) copy-start(f32[24,768]{1,0:T(8,128)S(1)} %get-tuple-element.550) | copy-start | bytes 221188 | tf_op jit(solution)/shard_map/while
  331.5 22.2 %copy-start.2 = (f32[24,768]{1,0:T(8,128)S(1)}, f32[24,768]{1,0:T(8,128)}, u32[]{:S(2)}) copy-start(f32[24,768]{1,0:T(8,128)} %get-tuple-element.554) | copy-start | bytes 221188 | tf_op jit(solution)/shard_map/while
  353.7 19.4 %copy-start.4 = (f32[24,768]{1,0:T(8,128)S(1)}, f32[24,768]{1,0:T(8,128)}, u32[]{:S(2)}) copy-start(f32[24,768]{1,0:T(8,128)} %copy-done.3) | copy-start | bytes 221188 | tf_op jit(solution)/shard_map/while
  357.4 15.6 %collective-permute-start = (f32[24,768]{1,0:T(8,128)S(1)}, f32[24,768]{1,0:T(8,128)S(1)}, u32[]{:S(2)}, u32[]{:S(2)}) collective-permute-start(f32[24,768]{1,0:T(8,128)S(1)} %get-tuple-element.502), channel_id=1, source_target_pairs={{0,16},{16,32},{32,48},{48,64},{64,80},{80,96},{96,112},{1,17},{17... | collective-permute-start | bytes 221192 | tf_op jit(solution)/shard_map/while/body/eval_jaxpr/ppermute | solution.py:14
  373.1 23.1 %copy-start.3 = (f32[24,768]{1,0:T(8,128)}, f32[24,768]{1,0:T(8,128)S(1)}, u32[]{:S(2)}) copy-start(f32[24,768]{1,0:T(8,128)S(1)} %get-tuple-element.550) | copy-start | bytes 221188 | tf_op jit(solution)/shard_map/while
  396.1 21.5 %copy-start.2 = (f32[24,768]{1,0:T(8,128)S(1)}, f32[24,768]{1,0:T(8,128)}, u32[]{:S(2)}) copy-start(f32[24,768]{1,0:T(8,128)} %get-tuple-element.554) | copy-start | bytes 221188 | tf_op jit(solution)/shard_map/while
  417.7 19.9 %copy-start.4 = (f32[24,768]{1,0:T(8,128)S(1)}, f32[24,768]{1,0:T(8,128)}, u32[]{:S(2)}) copy-start(f32[24,768]{1,0:T(8,128)} %copy-done.3) | copy-start | bytes 221188 | tf_op jit(solution)/shard_map/while
  421.4 16.2 %collective-permute-start = (f32[24,768]{1,0:T(8,128)S(1)}, f32[24,768]{1,0:T(8,128)S(1)}, u32[]{:S(2)}, u32[]{:S(2)}) collective-permute-start(f32[24,768]{1,0:T(8,128)S(1)} %get-tuple-element.502), channel_id=1, source_target_pairs={{0,16},{16,32},{32,48},{48,64},{64,80},{80,96},{96,112},{1,17},{17... | collective-permute-start | bytes 221192 | tf_op jit(solution)/shard_map/while/body/eval_jaxpr/ppermute | solution.py:14
  437.6 23.3 %copy-start.3 = (f32[24,768]{1,0:T(8,128)}, f32[24,768]{1,0:T(8,128)S(1)}, u32[]{:S(2)}) copy-start(f32[24,768]{1,0:T(8,128)S(1)} %get-tuple-element.550) | copy-start | bytes 221188 | tf_op jit(solution)/shard_map/while
  460.9 21.3 %copy-start.2 = (f32[24,768]{1,0:T(8,128)S(1)}, f32[24,768]{1,0:T(8,128)}, u32[]{:S(2)}) copy-start(f32[24,768]{1,0:T(8,128)} %get-tuple-element.554) | copy-start | bytes 221188 | tf_op jit(solution)/shard_map/while
  482.3 19.9 %copy-start.4 = (f32[24,768]{1,0:T(8,128)S(1)}, f32[24,768]{1,0:T(8,128)}, u32[]{:S(2)}) copy-start(f32[24,768]{1,0:T(8,128)} %copy-done.3) | copy-start | bytes 221188 | tf_op jit(solution)/shard_map/while
  486.0 16.1 %collective-permute-start = (f32[24,768]{1,0:T(8,128)S(1)}, f32[24,768]{1,0:T(8,128)S(1)}, u32[]{:S(2)}, u32[]{:S(2)}) collective-permute-start(f32[24,768]{1,0:T(8,128)S(1)} %get-tuple-element.502), channel_id=1, source_target_pairs={{0,16},{16,32},{32,48},{48,64},{64,80},{80,96},{96,112},{1,17},{17... | collective-permute-start | bytes 221192 | tf_op jit(solution)/shard_map/while/body/eval_jaxpr/ppermute | solution.py:14
  502.2 23.5 %copy-start.3 = (f32[24,768]{1,0:T(8,128)}, f32[24,768]{1,0:T(8,128)S(1)}, u32[]{:S(2)}) copy-start(f32[24,768]{1,0:T(8,128)S(1)} %get-tuple-element.550) | copy-start | bytes 221188 | tf_op jit(solution)/shard_map/while
  525.7 21.3 %copy-start.2 = (f32[24,768]{1,0:T(8,128)S(1)}, f32[24,768]{1,0:T(8,128)}, u32[]{:S(2)}) copy-start(f32[24,768]{1,0:T(8,128)} %get-tuple-element.554) | copy-start | bytes 221188 | tf_op jit(solution)/shard_map/while
  547.0 19.9 %copy-start.4 = (f32[24,768]{1,0:T(8,128)S(1)}, f32[24,768]{1,0:T(8,128)}, u32[]{:S(2)}) copy-start(f32[24,768]{1,0:T(8,128)} %copy-done.3) | copy-start | bytes 221188 | tf_op jit(solution)/shard_map/while
  550.7 16.2 %collective-permute-start = (f32[24,768]{1,0:T(8,128)S(1)}, f32[24,768]{1,0:T(8,128)S(1)}, u32[]{:S(2)}, u32[]{:S(2)}) collective-permute-start(f32[24,768]{1,0:T(8,128)S(1)} %get-tuple-element.502), channel_id=1, source_target_pairs={{0,16},{16,32},{32,48},{48,64},{64,80},{80,96},{96,112},{1,17},{17... | collective-permute-start | bytes 221192 | tf_op jit(solution)/shard_map/while/body/eval_jaxpr/ppermute | solution.py:14
  566.9 24.4 %copy-start.3 = (f32[24,768]{1,0:T(8,128)}, f32[24,768]{1,0:T(8,128)S(1)}, u32[]{:S(2)}) copy-start(f32[24,768]{1,0:T(8,128)S(1)} %get-tuple-element.550) | copy-start | bytes 221188 | tf_op jit(solution)/shard_map/while
  591.3 21.1 %copy-start.2 = (f32[24,768]{1,0:T(8,128)S(1)}, f32[24,768]{1,0:T(8,128)}, u32[]{:S(2)}) copy-start(f32[24,768]{1,0:T(8,128)} %get-tuple-element.554) | copy-start | bytes 221188 | tf_op jit(solution)/shard_map/while
  612.4 19.2 %copy-start.4 = (f32[24,768]{1,0:T(8,128)S(1)}, f32[24,768]{1,0:T(8,128)}, u32[]{:S(2)}) copy-start(f32[24,768]{1,0:T(8,128)} %copy-done.3) | copy-start | bytes 221188 | tf_op jit(solution)/shard_map/while
  616.2 15.5 %collective-permute-start = (f32[24,768]{1,0:T(8,128)S(1)}, f32[24,768]{1,0:T(8,128)S(1)}, u32[]{:S(2)}, u32[]{:S(2)}) collective-permute-start(f32[24,768]{1,0:T(8,128)S(1)} %get-tuple-element.502), channel_id=1, source_target_pairs={{0,16},{16,32},{32,48},{48,64},{64,80},{80,96},{96,112},{1,17},{17... | collective-permute-start | bytes 221192 | tf_op jit(solution)/shard_map/while/body/eval_jaxpr/ppermute | solution.py:14
  631.7 24.3 %copy-start.3 = (f32[24,768]{1,0:T(8,128)}, f32[24,768]{1,0:T(8,128)S(1)}, u32[]{:S(2)}) copy-start(f32[24,768]{1,0:T(8,128)S(1)} %get-tuple-element.550) | copy-start | bytes 221188 | tf_op jit(solution)/shard_map/while
  656.0 21.2 %copy-start.2 = (f32[24,768]{1,0:T(8,128)S(1)}, f32[24,768]{1,0:T(8,128)}, u32[]{:S(2)}) copy-start(f32[24,768]{1,0:T(8,128)} %get-tuple-element.554) | copy-start | bytes 221188 | tf_op jit(solution)/shard_map/while
  677.2 19.2 %copy-start.4 = (f32[24,768]{1,0:T(8,128)S(1)}, f32[24,768]{1,0:T(8,128)}, u32[]{:S(2)}) copy-start(f32[24,768]{1,0:T(8,128)} %copy-done.3) | copy-start | bytes 221188 | tf_op jit(solution)/shard_map/while
  680.9 15.5 %collective-permute-start = (f32[24,768]{1,0:T(8,128)S(1)}, f32[24,768]{1,0:T(8,128)S(1)}, u32[]{:S(2)}, u32[]{:S(2)}) collective-permute-start(f32[24,768]{1,0:T(8,128)S(1)} %get-tuple-element.502), channel_id=1, source_target_pairs={{0,16},{16,32},{32,48},{48,64},{64,80},{80,96},{96,112},{1,17},{17... | collective-permute-start | bytes 221192 | tf_op jit(solution)/shard_map/while/body/eval_jaxpr/ppermute | solution.py:14
  696.4 23.9 %copy-start.3 = (f32[24,768]{1,0:T(8,128)}, f32[24,768]{1,0:T(8,128)S(1)}, u32[]{:S(2)}) copy-start(f32[24,768]{1,0:T(8,128)S(1)} %get-tuple-element.550) | copy-start | bytes 221188 | tf_op jit(solution)/shard_map/while
  720.2 21.1 %copy-start.2 = (f32[24,768]{1,0:T(8,128)S(1)}, f32[24,768]{1,0:T(8,128)}, u32[]{:S(2)}) copy-start(f32[24,768]{1,0:T(8,128)} %get-tuple-element.554) | copy-start | bytes 221188 | tf_op jit(solution)/shard_map/while
  741.3 19.8 %copy-start.4 = (f32[24,768]{1,0:T(8,128)S(1)}, f32[24,768]{1,0:T(8,128)}, u32[]{:S(2)}) copy-start(f32[24,768]{1,0:T(8,128)} %copy-done.3) | copy-start | bytes 221188 | tf_op jit(solution)/shard_map/while
  745.0 16.1 %collective-permute-start = (f32[24,768]{1,0:T(8,128)S(1)}, f32[24,768]{1,0:T(8,128)S(1)}, u32[]{:S(2)}, u32[]{:S(2)}) collective-permute-start(f32[24,768]{1,0:T(8,128)S(1)} %get-tuple-element.502), channel_id=1, source_target_pairs={{0,16},{16,32},{32,48},{48,64},{64,80},{80,96},{96,112},{1,17},{17... | collective-permute-start | bytes 221192 | tf_op jit(solution)/shard_map/while/body/eval_jaxpr/ppermute | solution.py:14
  761.1 23.7 %copy-start.3 = (f32[24,768]{1,0:T(8,128)}, f32[24,768]{1,0:T(8,128)S(1)}, u32[]{:S(2)}) copy-start(f32[24,768]{1,0:T(8,128)S(1)} %get-tuple-element.550) | copy-start | bytes 221188 | tf_op jit(solution)/shard_map/while
  784.9 21.1 %copy-start.2 = (f32[24,768]{1,0:T(8,128)S(1)}, f32[24,768]{1,0:T(8,128)}, u32[]{:S(2)}) copy-start(f32[24,768]{1,0:T(8,128)} %get-tuple-element.554) | copy-start | bytes 221188 | tf_op jit(solution)/shard_map/while
  805.9 19.9 %copy-start.4 = (f32[24,768]{1,0:T(8,128)S(1)}, f32[24,768]{1,0:T(8,128)}, u32[]{:S(2)}) copy-start(f32[24,768]{1,0:T(8,128)} %copy-done.3) | copy-start | bytes 221188 | tf_op jit(solution)/shard_map/while
  809.7 16.2 %collective-permute-start = (f32[24,768]{1,0:T(8,128)S(1)}, f32[24,768]{1,0:T(8,128)S(1)}, u32[]{:S(2)}, u32[]{:S(2)}) collective-permute-start(f32[24,768]{1,0:T(8,128)S(1)} %get-tuple-element.502), channel_id=1, source_target_pairs={{0,16},{16,32},{32,48},{48,64},{64,80},{80,96},{96,112},{1,17},{17... | collective-permute-start | bytes 221192 | tf_op jit(solution)/shard_map/while/body/eval_jaxpr/ppermute | solution.py:14
  825.8 23.5 %copy-start.3 = (f32[24,768]{1,0:T(8,128)}, f32[24,768]{1,0:T(8,128)S(1)}, u32[]{:S(2)}) copy-start(f32[24,768]{1,0:T(8,128)S(1)} %get-tuple-element.550) | copy-start | bytes 221188 | tf_op jit(solution)/shard_map/while
  849.4 21.2 %copy-start.2 = (f32[24,768]{1,0:T(8,128)S(1)}, f32[24,768]{1,0:T(8,128)}, u32[]{:S(2)}) copy-start(f32[24,768]{1,0:T(8,128)} %get-tuple-element.554) | copy-start | bytes 221188 | tf_op jit(solution)/shard_map/while
  870.6 20.0 %copy-start.4 = (f32[24,768]{1,0:T(8,128)S(1)}, f32[24,768]{1,0:T(8,128)}, u32[]{:S(2)}) copy-start(f32[24,768]{1,0:T(8,128)} %copy-done.3) | copy-start | bytes 221188 | tf_op jit(solution)/shard_map/while
  874.3 16.3 %collective-permute-start = (f32[24,768]{1,0:T(8,128)S(1)}, f32[24,768]{1,0:T(8,128)S(1)}, u32[]{:S(2)}, u32[]{:S(2)}) collective-permute-start(f32[24,768]{1,0:T(8,128)S(1)} %get-tuple-element.502), channel_id=1, source_target_pairs={{0,16},{16,32},{32,48},{48,64},{64,80},{80,96},{96,112},{1,17},{17... | collective-permute-start | bytes 221192 | tf_op jit(solution)/shard_map/while/body/eval_jaxpr/ppermute | solution.py:14
  890.6 23.4 %copy-start.3 = (f32[24,768]{1,0:T(8,128)}, f32[24,768]{1,0:T(8,128)S(1)}, u32[]{:S(2)}) copy-start(f32[24,768]{1,0:T(8,128)S(1)} %get-tuple-element.550) | copy-start | bytes 221188 | tf_op jit(solution)/shard_map/while
  914.0 21.2 %copy-start.2 = (f32[24,768]{1,0:T(8,128)S(1)}, f32[24,768]{1,0:T(8,128)}, u32[]{:S(2)}) copy-start(f32[24,768]{1,0:T(8,128)} %get-tuple-element.554) | copy-start | bytes 221188 | tf_op jit(solution)/shard_map/while
  935.2 20.1 %copy-start.4 = (f32[24,768]{1,0:T(8,128)S(1)}, f32[24,768]{1,0:T(8,128)}, u32[]{:S(2)}) copy-start(f32[24,768]{1,0:T(8,128)} %copy-done.3) | copy-start | bytes 221188 | tf_op jit(solution)/shard_map/while
  938.9 16.4 %collective-permute-start = (f32[24,768]{1,0:T(8,128)S(1)}, f32[24,768]{1,0:T(8,128)S(1)}, u32[]{:S(2)}, u32[]{:S(2)}) collective-permute-start(f32[24,768]{1,0:T(8,128)S(1)} %get-tuple-element.502), channel_id=1, source_target_pairs={{0,16},{16,32},{32,48},{48,64},{64,80},{80,96},{96,112},{1,17},{17... | collective-permute-start | bytes 221192 | tf_op jit(solution)/shard_map/while/body/eval_jaxpr/ppermute | solution.py:14
  955.3 23.4 %copy-start.3 = (f32[24,768]{1,0:T(8,128)}, f32[24,768]{1,0:T(8,128)S(1)}, u32[]{:S(2)}) copy-start(f32[24,768]{1,0:T(8,128)S(1)} %get-tuple-element.550) | copy-start | bytes 221188 | tf_op jit(solution)/shard_map/while
  978.7 21.1 %copy-start.2 = (f32[24,768]{1,0:T(8,128)S(1)}, f32[24,768]{1,0:T(8,128)}, u32[]{:S(2)}) copy-start(f32[24,768]{1,0:T(8,128)} %get-tuple-element.554) | copy-start | bytes 221188 | tf_op jit(solution)/shard_map/while
  999.8 20.2 %copy-start.4 = (f32[24,768]{1,0:T(8,128)S(1)}, f32[24,768]{1,0:T(8,128)}, u32[]{:S(2)}) copy-start(f32[24,768]{1,0:T(8,128)} %copy-done.3) | copy-start | bytes 221188 | tf_op jit(solution)/shard_map/while
  1003.5 16.5 %collective-permute-start = (f32[24,768]{1,0:T(8,128)S(1)}, f32[24,768]{1,0:T(8,128)S(1)}, u32[]{:S(2)}, u32[]{:S(2)}) collective-permute-start(f32[24,768]{1,0:T(8,128)S(1)} %get-tuple-element.502), channel_id=1, source_target_pairs={{0,16},{16,32},{32,48},{48,64},{64,80},{80,96},{96,112},{1,17},{17... | collective-permute-start | bytes 221192 | tf_op jit(solution)/shard_map/while/body/eval_jaxpr/ppermute | solution.py:14
  1020.0 23.5 %copy-start.3 = (f32[24,768]{1,0:T(8,128)}, f32[24,768]{1,0:T(8,128)S(1)}, u32[]{:S(2)}) copy-start(f32[24,768]{1,0:T(8,128)S(1)} %get-tuple-element.550) | copy-start | bytes 221188 | tf_op jit(solution)/shard_map/while
  1043.5 21.4 %copy-start.2 = (f32[24,768]{1,0:T(8,128)S(1)}, f32[24,768]{1,0:T(8,128)}, u32[]{:S(2)}) copy-start(f32[24,768]{1,0:T(8,128)} %get-tuple-element.554) | copy-start | bytes 221188 | tf_op jit(solution)/shard_map/while
  1064.9 19.9 %copy-start.4 = (f32[24,768]{1,0:T(8,128)S(1)}, f32[24,768]{1,0:T(8,128)}, u32[]{:S(2)}) copy-start(f32[24,768]{1,0:T(8,128)} %copy-done.3) | copy-start | bytes 221188 | tf_op jit(solution)/shard_map/while
  1068.6 16.2 %collective-permute-start = (f32[24,768]{1,0:T(8,128)S(1)}, f32[24,768]{1,0:T(8,128)S(1)}, u32[]{:S(2)}, u32[]{:S(2)}) collective-permute-start(f32[24,768]{1,0:T(8,128)S(1)} %get-tuple-element.502), channel_id=1, source_target_pairs={{0,16},{16,32},{32,48},{48,64},{64,80},{80,96},{96,112},{1,17},{17... | collective-permute-start | bytes 221192 | tf_op jit(solution)/shard_map/while/body/eval_jaxpr/ppermute | solution.py:14
  (14 other events, 87.6 us)
Sparse Core Ops, SparseCore 0:
  27.4 69.8 reduce-scatter.3
where the time goes:
time: 1110 us; the launch traced here: 1100 us
  blocking collectives  567 us (51%)
  starting transfers between devices  215 us (19%)
  matrix products  152 us (14%)
  waiting for transfers between devices  65.6 us (6%)
  local copies, waits for them, and re-layouts  46.7 us (4%)
  other arithmetic  40.4 us (4%)
  between operations  14.1 us (1%)
    all_gather x15, blocking collectives, token_layer(): lax.all_gather(projected[:, width:2 * width], 'tok', axis=0, tiled=True)  282 us
    all_gather x15, blocking collectives, token_layer(): lax.all_gather(projected[:, 2 * width:], 'tok', axis=0, tiled=True)  245 us
    ppermute x15, starting transfers between devices, passed_along(): return lax.ppermute(x, axis, pairs)  215 us
    unnamed x2, waiting for transfers between devices  65.6 us
    dot_general x15, matrix products, token_layer(): gate_up = jnp.dot(normed_t, weight_ff, preferred_element_type=jnp.float32)  47.2 us
    dot_general x15, matrix products, token_layer(): jnp.dot(normed, weight_qkv, preferred_element_type=jnp.float32)  40.4 us
    dot_general x15, matrix products, token_layer(): jnp.dot(attended, weight_out, preferred_element_type=jnp.float32)  25 us
  transfers between devices with their start and end apart: 16, of which 1 were waited for; matrix products, arithmetic and copies ran while one was open for 3% of the time, Pallas kernels for 0%

commit v1 on v0

v1 whole, which is shorter than its diff:
```python
import jax
import jax.numpy as jnp
from jax import lax
from jax.experimental import pallas as pl
from jax.experimental.pallas import tpu as pltpu
from jax.sharding import PartitionSpec as P

HEADS = 16
HEAD_DIM = 48
FF = 1536
D = 768
POSES = 8
TOK_DEVS = 16
SECTIONS = 8
ROWS = 192
TOK_DEV = 24
ATOM_DEV = 216
ATOM_PAD = 224
COND_PAD = 32
KEYS = 384
GROUP = 384
MESH = pl.DeviceIdType.MESH
BF = jnp.bfloat16
F32 = jnp.float32


def chip_of(pose):
    x = pose // 2
    return 4 * x + 2 * (pose % 2) + x % 2


def normalise(v):
    centre = v - jnp.mean(v, axis=-1, keepdims=True)
    return centre * lax.rsqrt(jnp.mean(centre * centre, axis=-1, keepdims=True) + 1e-05)


def landed(ref, sem):
    pltpu.make_async_copy(ref, ref, sem).wait()


def kernel(
    coords_ref, atom_ref, count_ref, cond_ref, bias_ref, wcoord_ref, win_ref,
    wada_ref, wqkv_ref, wout_ref, wff_ref, wdown_ref,
    out_ref,
    c_src, a_src, d_src, c_all, a_all, n_all, d_all, b_all,
    wada_v, wqkv_v, wout_v, wff_v, wdown_v,
    cond, cond_tx, x, xin, xtx, norm, q, kv, att, hid, fin_tx, fin,
    c_send, c_recv, a_send, a_recv, n_send, n_recv, d_send, d_recv, b_send, b_recv,
    w_send, w_recv, ada_sem, m_send, m_recv, kv_send, kv_recv, x_send, x_recv, f_send, f_recv,
):
    s = lax.axis_index("section")
    t = lax.axis_index("tok")
    plane = s // 2
    core = lax.rem(s, 2)
    sibling = s + 1 - 2 * core
    cx, cz = t // 4, lax.rem(t, 4)
    active = lax.rem(cx + cz, 2) == 0
    pose = 2 * cx + cz // 2
    half = t // 8

    weights = ((wqkv_ref, wqkv_v), (wout_ref, wout_v), (wff_ref, wff_v), (wdown_ref, wdown_v))

    @pl.when(active)
    def _():
        pltpu.make_async_copy(wada_ref, wada_v, ada_sem).start()
        for k, (src, dst) in enumerate(weights):
            pltpu.make_async_copy(src, dst.at[core], w_recv.at[core, k]).start()

    barrier = pltpu.get_barrier_semaphore()

    def greet(section, tok):
        pl.semaphore_signal(barrier, inc=1, device_id=(section, tok), device_id_type=MESH)

    @pl.when(active)
    def _():
        @pl.loop(0, TOK_DEVS)
        def _(j):
            @pl.when(j != t)
            def _():
                greet(s, j)

        @pl.loop(0, 8)
        def _(j):
            greet(sibling, 8 * core + j)

        greet(sibling, t)

        @pl.when((s == 0) & (pose != 0))
        def _():
            @pl.loop(0, TOK_DEVS)
            def _(j):
                greet(pose, j)

        @pl.when((s == 1) & (pose != 1))
        def _():
            greet(pose, TOK_DEVS - 1)

        @pl.when(plane > 0)
        def _():
            greet(s - 2, t)

    fin_section, fin_tok = 6 + half, chip_of(s)
    fin_self = (fin_section == s) & (fin_tok == t)

    @pl.when(jnp.logical_not(fin_self))
    def _():
        greet(fin_section, fin_tok)

    c_src[...] = jnp.zeros_like(c_src)
    c_src[0:3, 0:ATOM_DEV] = coords_ref[0]
    a_src[...] = jnp.concatenate(
        [atom_ref[...].astype(F32), jnp.zeros((ATOM_PAD - ATOM_DEV, 128), F32)], axis=0
    ).astype(BF)
    d_src[...] = jnp.concatenate(
        [cond_ref[...].astype(F32), jnp.zeros((COND_PAD - TOK_DEV, D), F32)], axis=0
    ).astype(BF)

    one = lambda flag: flag.astype(jnp.int32)
    last = t == TOK_DEVS - 1
    expected = 8 - one(active)
    expected += 8 * one(half != core)
    expected += one(s != 0) + one(last & (s != 1))
    expected += one(active) + one(active & (plane < 3))
    fin_here = active & (plane == 3)
    fin_own = fin_here & (pose == s) & (half == core)
    expected += 8 * one(fin_here) - one(fin_own)
    pl.semaphore_wait(barrier, expected)

    def send(src, dst, send_sem, recv_sem, section, tok):
        own = (section == s) & (tok == t)

        @pl.when(own)
        def _():
            pltpu.make_async_copy(src, dst, recv_sem).start()

        @pl.when(jnp.logical_not(own))
        def _():
            pltpu.make_async_remote_copy(
                src_ref=src, dst_ref=dst, send_sem=send_sem, recv_sem=recv_sem,
                device_id=(section, tok), device_id_type=MESH,
            ).start()

    def sent(src, send_sem, section, tok):
        @pl.when(jnp.logical_not((section == s) & (tok == t)))
        def _():
            landed(src, send_sem)

    send(c_src, c_all.at[t], c_send.at[0], c_recv.at[t], 0, chip_of(s))

    @pl.when(last)
    def _():
        send(c_src, c_all.at[t], c_send.at[1], c_recv.at[t], 1, chip_of(s))

    @pl.when((s == 0) | ((s == 1) & last))
    def _():
        @pl.loop(0, POSES)
        def _(p):
            send(a_src, a_all.at[t], a_send.at[p], a_recv.at[t], s, chip_of(p))

    @pl.when((s == 0) & (t < 8))
    def _():
        @pl.loop(0, POSES)
        def _(p):
            send(count_ref, n_all.at[t], n_send.at[p], n_recv.at[t], s, chip_of(p))

    @pl.loop(0, POSES)
    def _(p):
        send(d_src, d_all.at[t], d_send.at[p], d_recv.at[t], s, chip_of(p))

    @pl.loop(0, POSES)
    def _(p):
        send(bias_ref, b_all.at[core, t - 8 * half], b_send.at[p], b_recv.at[core, t - 8 * half],
             2 * plane + half, chip_of(p))

    @pl.when(active)
    def _():
        for k, (src, dst) in enumerate(weights):
            pltpu.make_async_remote_copy(
                src_ref=src, dst_ref=dst.at[core], send_sem=w_send.at[k],
                recv_sem=w_recv.at[core, k], device_id=(sibling, t), device_id_type=MESH,
            ).start()

    def act_of(points, single):
        moved = lax.dot_general(
            points, wcoord_ref[...], (((0,), (0,)), ((), ())),
            precision=lax.Precision.HIGHEST, preferred_element_type=F32,
        )
        return jnp.maximum(single.astype(F32) + moved[:ATOM_PAD], 0.0)

    def enter_first():
        @pl.loop(0, 8)
        def _(j):
            landed(n_all.at[j], n_recv.at[j])

        counts = jnp.concatenate([n_all[j] for j in range(8)], axis=0)
        before = (
            lax.broadcasted_iota(jnp.int32, (ROWS, ROWS), 1)
            < lax.broadcasted_iota(jnp.int32, (ROWS, ROWS), 0)
        ).astype(F32).astype(BF)
        starts = jnp.dot(before, counts.astype(BF), preferred_element_type=F32)
        ends = starts + counts
        lower = jnp.concatenate([starts, starts], axis=1)[:, :ATOM_PAD]
        upper = jnp.concatenate([ends, ends], axis=1)[:, :ATOM_PAD]
        lane = lax.broadcasted_iota(jnp.int32, (ROWS, ATOM_PAD), 1)

        def block(j, pooled):
            landed(c_all.at[j], c_recv.at[j])
            landed(a_all.at[j], a_recv.at[j])
            place = (lane + j * ATOM_DEV).astype(F32)
            inside = (place >= lower) & (place < upper) & (lane < ATOM_DEV)
            member = jnp.where(inside, 1.0, 0.0).astype(BF)
            act = act_of(c_all[j], a_all[j]).astype(BF)
            return pooled + jnp.dot(member, act, preferred_element_type=F32)

        pooled = lax.fori_loop(0, TOK_DEVS, block, jnp.zeros((ROWS, 128), F32))
        averaged = (pooled / counts).astype(BF)
        x[...] = jnp.dot(averaged, win_ref[...], preferred_element_type=F32)

    def enter_second():
        j = TOK_DEVS - 1
        landed(c_all.at[j], c_recv.at[j])
        landed(a_all.at[j], a_recv.at[j])
        act = act_of(c_all[j], a_all[j])[ATOM_DEV - ROWS : ATOM_DEV]
        x[...] = jnp.dot(act.astype(BF), win_ref[...], preferred_element_type=F32)

    def conditions():
        @pl.loop(0, TOK_DEVS)
        def _(j):
            landed(d_all.at[j], d_recv.at[j])

        landed(wada_ref, ada_sem)

        def rows_for(which, store):
            rows = d_all[pl.ds(8 * which, 8)].reshape(8 * COND_PAD, D)
            for k in range(4):
                full = jnp.dot(
                    rows, wada_v[:, D * k : D * (k + 1)], preferred_element_type=F32
                )
                value = full.reshape(8, COND_PAD, D)[:, :TOK_DEV].reshape(ROWS, D)
                store(k, jax.nn.sigmoid(value) if k % 2 == 0 else value)

        def to_send(k, value):
            cond_tx[k] = value

        def to_keep(k, value):
            cond[core, k] = value

        rows_for(1 - core, to_send)
        pltpu.make_async_remote_copy(
            src_ref=cond_tx, dst_ref=cond.at[core], send_sem=m_send, recv_sem=m_recv,
            device_id=(sibling, t), device_id_type=MESH,
        ).start()
        rows_for(core, to_keep)

    own_rows = pl.ds(pl.multiple_of(core * ROWS, ROWS), ROWS)
    other_rows = pl.ds(pl.multiple_of((1 - core) * ROWS, ROWS), ROWS)

    def layer(lp):
        @pl.when(lp != core)
        def _():
            landed(cond.at[lp], m_recv)

        norm[...] = (normalise(x[...]) * cond[lp, 0] + cond[lp, 1]).astype(BF)
        landed(wqkv_v.at[lp], w_recv.at[lp, 0])

        def project(column, width):
            return jnp.dot(
                norm[...], wqkv_v[lp, :, column : column + width], preferred_element_type=F32
            ).astype(BF)

        for part in range(2):
            for j in range(3):
                kv[lp, part, own_rows, 256 * j : 256 * (j + 1)] = project(
                    D * (part + 1) + 256 * j, 256
                )
            pltpu.make_async_remote_copy(
                src_ref=kv.at[lp, part, own_rows], dst_ref=kv.at[lp, part, own_rows],
                send_sem=kv_send.at[lp, part], recv_sem=kv_recv.at[lp, part],
                device_id=(sibling, t), device_id_type=MESH,
            ).start()
        for j in range(3):
            q[:, 256 * j : 256 * (j + 1)] = project(256 * j, 256)

        @pl.loop(0, 8)
        def _(j):
            landed(b_all.at[lp, j], b_recv.at[lp, j])

        for part in range(2):
            landed(kv.at[lp, part, other_rows], kv_recv.at[lp, part])

        @pl.loop(0, 2)
        def _(g):
            blocks = [None, None, None]
            for pair in range(4):
                bias = b_all[lp, :, pl.ds(pl.multiple_of(192 * g + 48 * pair, 48), 48), :].astype(F32)
                for e in range(2):
                    low = HEAD_DIM * (2 * pair + e)
                    high = low + HEAD_DIM
                    first, stop = low // 128, (high + 127) // 128
                    width = 128 * (stop - first)
                    lanes = pl.ds(pl.multiple_of(g * GROUP + 128 * first, 128), width)
                    lane = lax.broadcasted_iota(jnp.int32, (1, width), 1) + 128 * first
                    mask = jnp.where((lane >= low) & (lane < high), 1.0, 0.0).astype(BF)
                    scores = lax.dot_general(
                        q[:, lanes] * mask, kv[lp, 0, :, lanes], (((1,), (1,)), ((), ())),
                        preferred_element_type=F32,
                    )
                    scores = scores * HEAD_DIM ** (-0.5) + bias[
                        :, TOK_DEV * e : TOK_DEV * (e + 1)
                    ].reshape(ROWS, KEYS)
                    top = jnp.max(scores, axis=-1, keepdims=True)
                    weight = jnp.exp(scores - top)
                    total = jnp.sum(weight, axis=-1, keepdims=True)
                    out = jnp.dot(
                        weight.astype(BF), kv[lp, 1, :, lanes], preferred_element_type=F32
                    ) / total
                    for b in range(first, stop):
                        piece = out[:, 128 * (b - first) : 128 * (b - first + 1)]
                        if blocks[b] is None:
                            blocks[b] = piece
                        else:
                            at = lax.broadcasted_iota(jnp.int32, (ROWS, 128), 1) + 128 * b
                            blocks[b] = jnp.where(at >= low, piece, blocks[b])
            for b in range(3):
                att[:, pl.ds(pl.multiple_of(g * GROUP + 128 * b, 128), 128)] = blocks[b].astype(BF)

        for part in range(2):
            landed(kv.at[lp, part, own_rows], kv_send.at[lp, part])

        landed(wout_v.at[lp], w_recv.at[lp, 1])
        for j in range(3):
            cols = slice(256 * j, 256 * (j + 1))
            x[:, cols] = x[:, cols] + jnp.dot(
                att[...], wout_v[lp, :, cols], preferred_element_type=F32
            )
        norm[...] = (normalise(x[...]) * cond[lp, 2] + cond[lp, 3]).astype(BF)
        landed(wff_v.at[lp], w_recv.at[lp, 2])
        for j in range(6):
            gate = jnp.dot(
                norm[...], wff_v[lp, :, 256 * j : 256 * (j + 1)], preferred_element_type=F32
            )
            up = jnp.dot(
                norm[...], wff_v[lp, :, FF + 256 * j : FF + 256 * (j + 1)],
                preferred_element_type=F32,
            )
            hid[:, 256 * j : 256 * (j + 1)] = (jax.nn.silu(gate) * up).astype(BF)
        landed(wdown_v.at[lp], w_recv.at[lp, 3])
        for j in range(3):
            cols = slice(256 * j, 256 * (j + 1))
            x[:, cols] = x[:, cols] + jnp.dot(
                hid[...], wdown_v[lp, :, cols], preferred_element_type=F32
            )

    @pl.when(active)
    def _():
        conditions()

        @pl.when(s == 0)
        def _():
            enter_first()

        @pl.when(s == 1)
        def _():
            enter_second()

        @pl.when(plane > 0)
        def _():
            landed(xin, x_recv)
            x[...] = xin[...].astype(F32)

        @pl.loop(0, 2)
        def _(lp):
            layer(lp)

        @pl.when(plane < 3)
        def _():
            xtx[...] = x[...].astype(BF)
            pltpu.make_async_remote_copy(
                src_ref=xtx, dst_ref=xin, send_sem=x_send, recv_sem=x_recv,
                device_id=(s + 2, t), device_id_type=MESH,
            ).start()

        @pl.when(plane == 3)
        def _():
            done = normalise(x[...]).reshape(8, TOK_DEV, D)
            fin_tx[...] = jnp.concatenate(
                [done, jnp.zeros((8, COND_PAD - TOK_DEV, D), F32)], axis=1
            ).astype(BF)

            @pl.loop(0, 8)
            def _(j):
                send(fin_tx.at[j], fin, f_send.at[j], f_recv, pose, 8 * core + j)

    landed(fin, f_recv)
    out_ref[...] = fin[...]

    sent(c_src, c_send.at[0], 0, chip_of(s))

    @pl.when(last)
    def _():
        sent(c_src, c_send.at[1], 1, chip_of(s))

    @pl.when((s == 0) | ((s == 1) & last))
    def _():
        @pl.loop(0, POSES)
        def _(p):
            sent(a_src, a_send.at[p], s, chip_of(p))

    @pl.when((s == 0) & (t < 8))
    def _():
        @pl.loop(0, POSES)
        def _(p):
            sent(count_ref, n_send.at[p], s, chip_of(p))

    @pl.loop(0, POSES)
    def _(p):
        sent(d_src, d_send.at[p], s, chip_of(p))
        sent(bias_ref, b_send.at[p], 2 * plane + half, chip_of(p))

    @pl.when(active)
    def _():
        for k, (src, dst) in enumerate(weights):
            landed(src, w_send.at[k])
        landed(cond_tx, m_send)

        @pl.when(plane < 3)
        def _():
            landed(xtx, x_send)

        @pl.when(plane == 3)
        def _():
            @pl.loop(0, 8)
            def _(j):
                sent(fin_tx.at[j], f_send.at[j], pose, 8 * core + j)


def body(
    coords, atom_single, token_atoms, cond_single, pair_bias, w_coord, w_in,
    w_ada, w_qkv, w_out, w_ff, w_down,
):
    counts = jnp.broadcast_to(token_atoms.astype(F32)[:, None], (TOK_DEV, 128))
    bias = pair_bias[0].reshape(HEADS * TOK_DEV, KEYS)
    w_coord_rows = jnp.concatenate([w_coord, jnp.zeros((5, 128), F32)], axis=0)
    vmem = pl.BlockSpec(memory_space=pltpu.VMEM)
    hbm = pl.BlockSpec(memory_space=pl.ANY)
    dma = pltpu.SemaphoreType.DMA
    rows = pl.pallas_call(
        kernel,
        out_shape=jax.ShapeDtypeStruct((COND_PAD, D), BF),
        in_specs=[vmem, vmem, vmem, vmem, hbm, vmem, vmem, hbm, hbm, hbm, hbm, hbm],
        out_specs=vmem,
        scratch_shapes=[
            pltpu.VMEM((8, 256), F32),
            pltpu.VMEM((ATOM_PAD, 128), BF),
            pltpu.VMEM((COND_PAD, D), BF),
            pltpu.VMEM((TOK_DEVS, 8, 256), F32),
            pltpu.VMEM((TOK_DEVS, ATOM_PAD, 128), BF),
            pltpu.VMEM((8, TOK_DEV, 128), F32),
            pltpu.VMEM((TOK_DEVS, COND_PAD, D), BF),
            pltpu.VMEM((2, 8, HEADS * TOK_DEV, KEYS), BF),
            pltpu.VMEM((D, 4 * D), BF),
            pltpu.VMEM((2, D, 3 * D), BF),
            pltpu.VMEM((2, D, D), BF),
            pltpu.VMEM((2, D, 2 * FF), BF),
            pltpu.VMEM((2, FF, D), BF),
            pltpu.VMEM((2, 4, ROWS, D), F32),
            pltpu.VMEM((4, ROWS, D), F32),
            pltpu.VMEM((ROWS, D), F32),
            pltpu.VMEM((ROWS, D), BF),
            pltpu.VMEM((ROWS, D), BF),
            pltpu.VMEM((ROWS, D), BF),
            pltpu.VMEM((ROWS, D), BF),
            pltpu.VMEM((2, 2, KEYS, D), BF),
            pltpu.VMEM((ROWS, D), BF),
            pltpu.VMEM((ROWS, FF), BF),
            pltpu.VMEM((8, COND_PAD, D), BF),
            pltpu.VMEM((COND_PAD, D), BF),
            dma((2,)), dma((TOK_DEVS,)),
            dma((POSES,)), dma((TOK_DEVS,)),
            dma((POSES,)), dma((8,)),
            dma((POSES,)), dma((TOK_DEVS,)),
            dma((POSES,)), dma((2, 8)),
            dma((4,)), dma((2, 4)),
            dma,
            dma, dma,
            dma((2, 2)), dma((2, 2)),
            dma, dma,
            dma((8,)), dma,
        ],
        compiler_params=pltpu.CompilerParams(
            collective_id=0, has_side_effects=True, vmem_limit_bytes=60 << 20
        ),
    )(
        coords, atom_single, counts, cond_single, bias, w_coord_rows, w_in,
        w_ada[0], w_qkv[0], w_out[0], w_ff[0], w_down[0],
    )
    return rows[None, :TOK_DEV]


def solution(mesh):
    return jax.shard_map(
        body,
        mesh=mesh,
        in_specs=(
            P("section", None, "tok"),
            P("tok", None),
            P("tok"),
            P("tok", None),
            P("section", None, "tok", None),
            P(),
            P(),
            P("section", None, None),
            P("section", None, None),
            P("section", None, None),
            P("section", None, None),
            P("section", None, None),
        ),
        out_specs=P("section", "tok", None),
        check_vma=False,
    )
```

time: 1110 us -> 191 us (0.17)
  blocking collectives: 567 us -> 0 us
  starting transfers between devices: 215 us -> 0 us
  Pallas kernels: 0 us -> 184 us
  matrix products: 152 us -> 0 us
  waiting for transfers between devices: 65.6 us -> 0 us
  local copies, waits for them, and re-layouts: 46.7 us -> 4.61 us
  other arithmetic: 40.4 us -> 0.66 us
  between operations: 14.1 us -> 0.01 us
    all_gather x31 -> x0, blocking collectives: 543 us -> none  [the longest x15 282 us: token_layer(): lax.all_gather(projected[:, width:2 * width], 'tok', axis=0, tiled=True)]
    ppermute x15 -> x0, starting transfers between devices: 215 us -> none  [passed_along(): return lax.ppermute(x, axis, pairs)]
    pallas_call x0 -> x1, Pallas kernels: none -> 184 us  [body(): pl.pallas_call(kernel, out_shape=jax.ShapeDtypeStruct((COND_PAD, D), BF),...]
    dot_general x93 -> x0, matrix products: 152 us -> none  [the longest x15 47.2 us: token_layer(): gate_up = jnp.dot(normed_t, weight_ff, preferred_element_type=jnp.float32)]
    unnamed x2 -> x0, waiting for transfers between devices: 65.6 us -> none
    reduce_sum x61 -> x0, other arithmetic: 24.2 us -> none  [the longest x15 15.5 us: layer_norm(): centre = values - jnp.mean(values, axis=-1, keepdims=True)]
    convert_element_type x30 -> x0, local copies, waits for them, and re-layouts: 18 us -> none  [token_layer(): attended = attended.reshape(tok_dev, width).astype(jnp.bfloat16)]
    unnamed x1 -> x0, blocking collectives: 13.7 us -> none
  transfers between devices with their start and end apart: 16 -> 0, of which waited for: 1 -> 0; matrix products, arithmetic and copies ran while one was open for 3% -> 0% of each run, Pallas kernels for 0% -> 0%
where the time goes in v1:
time: 191 us; the launch traced here: 189 us
  Pallas kernels  184 us (96%)
  local copies, waits for them, and re-layouts  4.61 us (2%)
    pallas_call x1, Pallas kernels, body(): pl.pallas_call(kernel, out_shape=jax.ShapeDtypeStruct((COND_PAD, D), BF),...  184 us

profile of v1, /device:TPU:17, one launch (start us, length us, event | category | flops | bytes accessed | tf_op | source)
XLA Modules:
  0.0 189.3 jit_solution(15235900212090621953)
XLA Ops:
  0.0 0.7 convert_element_type.3
  0.7 1.3 copy.13.coords_ref
  1.9 1.3 concatenate.3.wcoord_ref
  3.2 0.7 broadcast_in_dim.4.count_ref
  3.9 184.0 %shard_map.118 = bf16[32,768]{1,0:T(8,128)(2,1)} custom-call(f32[1,3,216]{2,1,0:T(4,128)} %copy.13.coords_ref, bf16[216,128]{1,0:T(8,128)(2,1)} %atom_ref.1, f32[24,128]{1,0:T(8,128)} %broadcast_in_dim.4.count_ref, bf16[24,768]{1,0:T(8,128)(2,1)} %cond_ref.1, bf16[384,384]{1,0:T(8,128)(2,1)} %bitcast.13, f32[8,128]{1,0:T(8,128)} %concatenate.3.wcoord_ref, ...), custom_call_target="tpu_custom_call" | custom-call | tf_op jit(solution)/shard_map/pallas_call | solution.py:447
  187.9 1.4 slice_bitcast_fusion

commit v2 on v1

--- a/solution.py
+++ b/solution.py
@@ -42,10 +42,10 @@
     coords_ref, atom_ref, count_ref, cond_ref, bias_ref, wcoord_ref, win_ref,
     wada_ref, wqkv_ref, wout_ref, wff_ref, wdown_ref,
     out_ref,
-    c_src, a_src, d_src, c_all, a_all, n_all, d_all, b_all,
+    c_src, a_src, d_src, wc, c_all, a_all, d_all, b_all, relay,
     wada_v, wqkv_v, wout_v, wff_v, wdown_v,
     cond, cond_tx, x, xin, xtx, norm, q, kv, att, hid, fin_tx, fin,
-    c_send, c_recv, a_send, a_recv, n_send, n_recv, d_send, d_recv, b_send, b_recv,
+    c_send, c_recv, a_send, a_recv, d_send, d_recv, r_send, r_recv, b_send, b_recv, go,
     w_send, w_recv, ada_sem, m_send, m_recv, kv_send, kv_recv, x_send, x_recv, f_send, f_recv,
 ):
     s = lax.axis_index("section")
@@ -79,11 +79,9 @@
             def _():
                 greet(s, j)
 
-        @pl.loop(0, 8)
+        @pl.loop(0, TOK_DEVS)
         def _(j):
-            greet(sibling, 8 * core + j)
-
-        greet(sibling, t)
+            greet(sibling, j)
 
         @pl.when((s == 0) & (pose != 0))
         def _():
@@ -99,6 +97,13 @@
         def _():
             greet(s - 2, t)
 
+    greet(sibling, t)
+
+    @pl.loop(1, 4)
+    def _(k):
+        greet(s, 4 * lax.rem(cx + k, 4) + cz)
+        greet(s, 4 * cx + lax.rem(cz + k, 4))
+
     fin_section, fin_tok = 6 + half, chip_of(s)
     fin_self = (fin_section == s) & (fin_tok == t)
 
@@ -107,7 +112,10 @@
         greet(fin_section, fin_tok)
 
     c_src[...] = jnp.zeros_like(c_src)
-    c_src[0:3, 0:ATOM_DEV] = coords_ref[0]
+    c_src[0:3, 0:ATOM_DEV] = coords_ref[...].reshape(3, ATOM_DEV)
+    c_src[3:4, 0:TOK_DEV] = count_ref[...].astype(F32)
+    wc[...] = jnp.zeros_like(wc)
+    wc[0:3] = wcoord_ref[...]
     a_src[...] = jnp.concatenate(
         [atom_ref[...].astype(F32), jnp.zeros((ATOM_PAD - ATOM_DEV, 128), F32)], axis=0
     ).astype(BF)
@@ -118,9 +126,9 @@
     one = lambda flag: flag.astype(jnp.int32)
     last = t == TOK_DEVS - 1
     expected = 8 - one(active)
-    expected += 8 * one(half != core)
+    expected += 8 + 1 + 6
     expected += one(s != 0) + one(last & (s != 1))
-    expected += one(active) + one(active & (plane < 3))
+    expected += one(active & (plane < 3))
     fin_here = active & (plane == 3)
     fin_own = fin_here & (pose == s) & (half == core)
     expected += 8 * one(fin_here) - one(fin_own)
@@ -157,20 +165,66 @@
         def _(p):
             send(a_src, a_all.at[t], a_send.at[p], a_recv.at[t], s, chip_of(p))
 
-    @pl.when((s == 0) & (t < 8))
-    def _():
-        @pl.loop(0, POSES)
-        def _(p):
-            send(count_ref, n_all.at[t], n_send.at[p], n_recv.at[t], s, chip_of(p))
-
     @pl.loop(0, POSES)
     def _(p):
         send(d_src, d_all.at[t], d_send.at[p], d_recv.at[t], s, chip_of(p))
 
-    @pl.loop(0, POSES)
-    def _(p):
-        send(bias_ref, b_all.at[core, t - 8 * half], b_send.at[p], b_recv.at[core, t - 8 * half],
-             2 * plane + half, chip_of(p))
+    def legs(part, at, k):
+        if part == 0:
+            return 4 * lax.rem(cx + k, 4) + cz
+        return 4 * cx + lax.rem(cz + k, 4)
+
+    def half_of(part):
+        return bias_ref.at[pl.ds(ROWS * part, ROWS)]
+
+    def forward(part, at, source, act):
+        origin = 4 * at + cz if part == 0 else 4 * cx + at
+        block = lax.rem(origin, 8)
+        for e in range(2):
+            if part == 0:
+                tok = 4 * cx + lax.rem(cx, 2) + 2 * e
+            else:
+                tok = 4 * (lax.rem(cz, 2) + 2 * e) + cz
+            act(source, b_all.at[core, block, pl.ds(ROWS * part, ROWS)], b_send.at[part, at, e],
+                b_recv.at[core, block, part], 2 * plane + origin // 8, tok)
+
+    def bias_out():
+        for part in range(2):
+            here = cx if part == 0 else cz
+
+            @pl.loop(1, 4)
+            def _(k):
+                pltpu.make_async_remote_copy(
+                    src_ref=half_of(part), dst_ref=relay.at[part, here],
+                    send_sem=r_send.at[part, k], recv_sem=r_recv.at[part, here],
+                    device_id=(s, legs(part, here, k)), device_id_type=MESH,
+                ).start()
+
+        for part in range(2):
+            forward(part, cx if part == 0 else cz, half_of(part), send)
+
+    def bias_on():
+        @pl.loop(1, 4)
+        def _(k):
+            for part in range(2):
+                at = lax.rem((cx if part == 0 else cz) + k, 4)
+                landed(relay.at[part, at], r_recv.at[part, at])
+                forward(part, at, relay.at[part, at], send)
+
+    def bias_gone():
+        def gone(source, target, send_sem, recv_sem, section, tok):
+            sent(source, send_sem, section, tok)
+
+        for part in range(2):
+            @pl.loop(0, 4)
+            def _(k):
+                at = lax.rem((cx if part == 0 else cz) + k, 4)
+
+                @pl.when(k > 0)
+                def _():
+                    landed(half_of(part), r_send.at[part, k])
+
+                forward(part, at, half_of(part), gone)
 
     @pl.when(active)
     def _():
@@ -180,31 +234,54 @@
                 recv_sem=w_recv.at[core, k], device_id=(sibling, t), device_id_type=MESH,
             ).start()
 
+    @pl.when(core == 0)
+    def _():
+        bias_out()
+        bias_on()
+
+    @pl.when((core == 0) & jnp.logical_not(active))
+    def _():
+        bias_gone()
+        pl.semaphore_signal(go, inc=1, device_id=(sibling, t), device_id_type=MESH)
+
+    @pl.when((core == 1) & jnp.logical_not(active))
+    def _():
+        pl.semaphore_wait(go, 1)
+        bias_out()
+        bias_on()
+        bias_gone()
+
     def act_of(points, single):
         moved = lax.dot_general(
-            points, wcoord_ref[...], (((0,), (0,)), ((), ())),
+            points, wc[...], (((0,), (0,)), ((), ())),
             precision=lax.Precision.HIGHEST, preferred_element_type=F32,
         )
         return jnp.maximum(single.astype(F32) + moved[:ATOM_PAD], 0.0)
 
     def enter_first():
-        @pl.loop(0, 8)
+        @pl.loop(0, TOK_DEVS)
         def _(j):
-            landed(n_all.at[j], n_recv.at[j])
-
-        counts = jnp.concatenate([n_all[j] for j in range(8)], axis=0)
-        before = (
-            lax.broadcasted_iota(jnp.int32, (ROWS, ROWS), 1)
-            < lax.broadcasted_iota(jnp.int32, (ROWS, ROWS), 0)
-        ).astype(F32).astype(BF)
-        starts = jnp.dot(before, counts.astype(BF), preferred_element_type=F32)
+            landed(c_all.at[j], c_recv.at[j])
+
+        lane8 = lax.broadcasted_iota(jnp.int32, (TOK_DEV, 128), 1)
+        place8 = lax.broadcasted_iota(jnp.int32, (TOK_DEV, 128), 0)
+        count_blocks, start_blocks = [], []
+        total = jnp.zeros((TOK_DEV, 1), F32)
+        for j in range(8):
+            row = jnp.broadcast_to(c_all[j, 3:4, 0:128], (TOK_DEV, 128))
+            mine = jnp.where(lane8 == place8, row, 0.0)
+            ahead = jnp.where(lane8 < place8, row, 0.0)
+            count_blocks.append(jnp.sum(mine, axis=1, keepdims=True))
+            start_blocks.append(total + jnp.sum(ahead, axis=1, keepdims=True))
+            total = total + jnp.sum(row, axis=1, keepdims=True)
+        counts = jnp.broadcast_to(jnp.concatenate(count_blocks, axis=0), (ROWS, 128))
+        starts = jnp.broadcast_to(jnp.concatenate(start_blocks, axis=0), (ROWS, 128))
         ends = starts + counts
         lower = jnp.concatenate([starts, starts], axis=1)[:, :ATOM_PAD]
         upper = jnp.concatenate([ends, ends], axis=1)[:, :ATOM_PAD]
         lane = lax.broadcasted_iota(jnp.int32, (ROWS, ATOM_PAD), 1)
 
         def block(j, pooled):
-            landed(c_all.at[j], c_recv.at[j])
             landed(a_all.at[j], a_recv.at[j])
             place = (lane + j * ATOM_DEV).astype(F32)
             inside = (place >= lower) & (place < upper) & (lane < ATOM_DEV)
@@ -281,9 +358,14 @@
         for j in range(3):
             q[:, 256 * j : 256 * (j + 1)] = project(256 * j, 256)
 
-        @pl.loop(0, 8)
+        @pl.loop(0, 16)
         def _(j):
-            landed(b_all.at[lp, j], b_recv.at[lp, j])
+            block = b_all.at[lp, j // 2, pl.ds(ROWS * lax.rem(j, 2), ROWS)]
+            landed(block, b_recv.at[lp, j // 2, lax.rem(j, 2)])
+
+        @pl.when((lp == 0) & (core == 1))
+        def _():
+            bias_out()
 
         for part in range(2):
             landed(kv.at[lp, part, other_rows], kv_recv.at[lp, part])
@@ -324,6 +406,10 @@
             for b in range(3):
                 att[:, pl.ds(pl.multiple_of(g * GROUP + 128 * b, 128), 128)] = blocks[b].astype(BF)
 
+        @pl.when((lp == 0) & (core == 1))
+        def _():
+            bias_on()
+
         for part in range(2):
             landed(kv.at[lp, part, own_rows], kv_send.at[lp, part])
 
@@ -392,7 +478,7 @@
                 send(fin_tx.at[j], fin, f_send.at[j], f_recv, pose, 8 * core + j)
 
     landed(fin, f_recv)
-    out_ref[...] = fin[...]
+    out_ref[...] = fin[...].astype(F32)[:TOK_DEV].astype(BF)
 
     sent(c_src, c_send.at[0], 0, chip_of(s))
 
@@ -406,22 +492,16 @@
         def _(p):
             sent(a_src, a_send.at[p], s, chip_of(p))
 
-    @pl.when((s == 0) & (t < 8))
-    def _():
-        @pl.loop(0, POSES)
-        def _(p):
-            sent(count_ref, n_send.at[p], s, chip_of(p))
-
     @pl.loop(0, POSES)
     def _(p):
         sent(d_src, d_send.at[p], s, chip_of(p))
-        sent(bias_ref, b_send.at[p], 2 * plane + half, chip_of(p))
 
     @pl.when(active)
     def _():
         for k, (src, dst) in enumerate(weights):
             landed(src, w_send.at[k])
         landed(cond_tx, m_send)
+        bias_gone()
 
         @pl.when(plane < 3)
         def _():
@@ -438,26 +518,27 @@
     coords, atom_single, token_atoms, cond_single, pair_bias, w_coord, w_in,
     w_ada, w_qkv, w_out, w_ff, w_down,
 ):
-    counts = jnp.broadcast_to(token_atoms.astype(F32)[:, None], (TOK_DEV, 128))
+    counts = token_atoms.reshape(1, TOK_DEV)
+    points = jnp.transpose(coords, (1, 0, 2))
     bias = pair_bias[0].reshape(HEADS * TOK_DEV, KEYS)
-    w_coord_rows = jnp.concatenate([w_coord, jnp.zeros((5, 128), F32)], axis=0)
     vmem = pl.BlockSpec(memory_space=pltpu.VMEM)
     hbm = pl.BlockSpec(memory_space=pl.ANY)
     dma = pltpu.SemaphoreType.DMA
     rows = pl.pallas_call(
         kernel,
-        out_shape=jax.ShapeDtypeStruct((COND_PAD, D), BF),
+        out_shape=jax.ShapeDtypeStruct((TOK_DEV, D), BF),
         in_specs=[vmem, vmem, vmem, vmem, hbm, vmem, vmem, hbm, hbm, hbm, hbm, hbm],
         out_specs=vmem,
         scratch_shapes=[
             pltpu.VMEM((8, 256), F32),
             pltpu.VMEM((ATOM_PAD, 128), BF),
             pltpu.VMEM((COND_PAD, D), BF),
+            pltpu.VMEM((8, 128), F32),
             pltpu.VMEM((TOK_DEVS, 8, 256), F32),
             pltpu.VMEM((TOK_DEVS, ATOM_PAD, 128), BF),
-            pltpu.VMEM((8, TOK_DEV, 128), F32),
             pltpu.VMEM((TOK_DEVS, COND_PAD, D), BF),
             pltpu.VMEM((2, 8, HEADS * TOK_DEV, KEYS), BF),
+            pltpu.VMEM((2, 4, ROWS, KEYS), BF),
             pltpu.VMEM((D, 4 * D), BF),
             pltpu.VMEM((2, D, 3 * D), BF),
             pltpu.VMEM((2, D, D), BF),
@@ -477,9 +558,10 @@
             pltpu.VMEM((COND_PAD, D), BF),
             dma((2,)), dma((TOK_DEVS,)),
             dma((POSES,)), dma((TOK_DEVS,)),
-            dma((POSES,)), dma((8,)),
             dma((POSES,)), dma((TOK_DEVS,)),
-            dma((POSES,)), dma((2, 8)),
+            dma((2, 4)), dma((2, 4)),
+            dma((2, 4, 2)), dma((2, 8, 2)),
+            pltpu.SemaphoreType.REGULAR,
             dma((4,)), dma((2, 4)),
             dma,
             dma, dma,
@@ -491,10 +573,10 @@
             collective_id=0, has_side_effects=True, vmem_limit_bytes=60 << 20
         ),
     )(
-        coords, atom_single, counts, cond_single, bias, w_coord_rows, w_in,
+        points, atom_single, counts, cond_single, bias, w_coord, w_in,
         w_ada[0], w_qkv[0], w_out[0], w_ff[0], w_down[0],
     )
-    return rows[None, :TOK_DEV]
+    return rows[None]
 
 
 def solution(mesh):

time: 191 us -> 172 us (0.901)
  Pallas kernels: 184 us -> 169 us
  local copies, waits for them, and re-layouts: 4.61 us -> 1.39 us
    pallas_call x1, Pallas kernels: 184 us -> 169 us  [body(): pl.pallas_call(kernel, out_shape=jax.ShapeDtypeStruct((TOK_DEV, D), BF),...]
    broadcast_in_dim x2 -> x0, local copies, waits for them, and re-layouts: 2.06 us -> none  [the longest x1 1.39 us: body(): return rows[None, :TOK_DEV]]
where the time goes in v2:
time: 172 us; the launch traced here: 170 us
  Pallas kernels  169 us (98%)
    pallas_call x1, Pallas kernels, body(): pl.pallas_call(kernel, out_shape=jax.ShapeDtypeStruct((TOK_DEV, D), BF),...  169 us

profile of v2, /device:TPU:17, one launch (start us, length us, event | category | flops | bytes accessed | tf_op | source)
XLA Modules:
  0.0 170.4 jit_solution(16859087204033330970)
XLA Ops:
  0.0 169.1 %shard_map.118 = bf16[24,768]{1,0:T(8,128)(2,1)} custom-call(f32[3,1,216]{2,1,0:T(1,128)} %bitcast.16, bf16[216,128]{1,0:T(8,128)(2,1)} %atom_ref.1, s32[1,24]{1,0:T(1,128)} %bitcast.17, bf16[24,768]{1,0:T(8,128)(2,1)} %cond_ref.1, bf16[384,384]{1,0:T(8,128)(2,1)} %bitcast.14, f32[3,128]{1,0:T(4,128)} %wcoord_ref.1, bf16[128,768]{1,0:T(8,128)(2,1)} %win_ref.1, ...), custom_call_target="tpu_custom_call" | custom-call | tf_op jit(solution)/shard_map/pallas_call | solution.py:527
  169.1 1.4 copy.14

commit v3 on v2

--- a/solution.py
+++ b/solution.py
@@ -45,6 +45,7 @@
     c_src, a_src, d_src, wc, c_all, a_all, d_all, b_all, relay,
     wada_v, wqkv_v, wout_v, wff_v, wdown_v,
     cond, cond_tx, x, xin, xtx, norm, q, kv, att, hid, fin_tx, fin,
+    spread, scores, probs, inverse,
     c_send, c_recv, a_send, a_recv, d_send, d_recv, r_send, r_recv, b_send, b_recv, go,
     w_send, w_recv, ada_sem, m_send, m_recv, kv_send, kv_recv, x_send, x_recv, f_send, f_recv,
 ):
@@ -200,10 +201,10 @@
                     device_id=(s, legs(part, here, k)), device_id_type=MESH,
                 ).start()
 
+    def bias_on():
         for part in range(2):
             forward(part, cx if part == 0 else cz, half_of(part), send)
 
-    def bias_on():
         @pl.loop(1, 4)
         def _(k):
             for part in range(2):
@@ -234,9 +235,10 @@
                 recv_sem=w_recv.at[core, k], device_id=(sibling, t), device_id_type=MESH,
             ).start()
 
+    bias_out()
+
     @pl.when(core == 0)
     def _():
-        bias_out()
         bias_on()
 
     @pl.when((core == 0) & jnp.logical_not(active))
@@ -247,7 +249,6 @@
     @pl.when((core == 1) & jnp.logical_not(active))
     def _():
         pl.semaphore_wait(go, 1)
-        bias_out()
         bias_on()
         bias_gone()
 
@@ -363,52 +364,54 @@
             block = b_all.at[lp, j // 2, pl.ds(ROWS * lax.rem(j, 2), ROWS)]
             landed(block, b_recv.at[lp, j // 2, lax.rem(j, 2)])
 
-        @pl.when((lp == 0) & (core == 1))
-        def _():
-            bias_out()
-
         for part in range(2):
             landed(kv.at[lp, part, other_rows], kv_recv.at[lp, part])
 
-        @pl.loop(0, 2)
-        def _(g):
-            blocks = [None, None, None]
-            for pair in range(4):
-                bias = b_all[lp, :, pl.ds(pl.multiple_of(192 * g + 48 * pair, 48), 48), :].astype(F32)
-                for e in range(2):
-                    low = HEAD_DIM * (2 * pair + e)
-                    high = low + HEAD_DIM
-                    first, stop = low // 128, (high + 127) // 128
-                    width = 128 * (stop - first)
-                    lanes = pl.ds(pl.multiple_of(g * GROUP + 128 * first, 128), width)
-                    lane = lax.broadcasted_iota(jnp.int32, (1, width), 1) + 128 * first
-                    mask = jnp.where((lane >= low) & (lane < high), 1.0, 0.0).astype(BF)
-                    scores = lax.dot_general(
-                        q[:, lanes] * mask, kv[lp, 0, :, lanes], (((1,), (1,)), ((), ())),
-                        preferred_element_type=F32,
-                    )
-                    scores = scores * HEAD_DIM ** (-0.5) + bias[
-                        :, TOK_DEV * e : TOK_DEV * (e + 1)
-                    ].reshape(ROWS, KEYS)
-                    top = jnp.max(scores, axis=-1, keepdims=True)
-                    weight = jnp.exp(scores - top)
-                    total = jnp.sum(weight, axis=-1, keepdims=True)
-                    out = jnp.dot(
-                        weight.astype(BF), kv[lp, 1, :, lanes], preferred_element_type=F32
-                    ) / total
-                    for b in range(first, stop):
-                        piece = out[:, 128 * (b - first) : 128 * (b - first + 1)]
-                        if blocks[b] is None:
-                            blocks[b] = piece
-                        else:
-                            at = lax.broadcasted_iota(jnp.int32, (ROWS, 128), 1) + 128 * b
-                            blocks[b] = jnp.where(at >= low, piece, blocks[b])
-            for b in range(3):
-                att[:, pl.ds(pl.multiple_of(g * GROUP + 128 * b, 128), 128)] = blocks[b].astype(BF)
-
-        @pl.when((lp == 0) & (core == 1))
-        def _():
-            bias_on()
+        for w in range(3):
+            lanes = slice(256 * w, 256 * (w + 1))
+            window = q[:, lanes]
+            lane = lax.broadcasted_iota(jnp.int32, (1, 256), 1) + 256 * w
+            for k in range(6):
+                low = HEAD_DIM * (5 * w + k)
+                mask = jnp.where((lane >= low) & (lane < low + HEAD_DIM), 1.0, 0.0).astype(BF)
+                spread[ROWS * k : ROWS * (k + 1)] = window * mask
+            scores[w] = lax.dot_general(
+                spread[...], kv[lp, 0, :, lanes], (((1,), (1,)), ((), ())),
+                preferred_element_type=F32,
+            )
+
+        for pair in range(8):
+            bias = b_all[lp, :, 48 * pair : 48 * (pair + 1), :].astype(F32)
+            for e in range(2):
+                head = 2 * pair + e
+                w = min(head // 5, 2)
+                k = head - 5 * w
+                raw = scores[w, ROWS * k : ROWS * (k + 1)]
+                if k == 0 and w > 0:
+                    raw = raw + scores[w - 1, 5 * ROWS : 6 * ROWS]
+                logits = raw * HEAD_DIM ** (-0.5) + bias[
+                    :, TOK_DEV * e : TOK_DEV * (e + 1)
+                ].reshape(ROWS, KEYS)
+                top = jnp.max(logits, axis=-1, keepdims=True)
+                weight = jnp.exp(logits - top)
+                total = jnp.sum(weight, axis=-1, keepdims=True)
+                inverse[head] = jnp.broadcast_to(1.0 / total, (ROWS, 128))
+                probs[ROWS * head : ROWS * (head + 1)] = weight.astype(BF)
+
+        for w in range(3):
+            lanes = slice(256 * w, 256 * (w + 1))
+            out = jnp.dot(
+                probs[ROWS * 5 * w : ROWS * (5 * w + 6)], kv[lp, 1, :, lanes],
+                preferred_element_type=F32,
+            )
+            lane = lax.broadcasted_iota(jnp.int32, (1, 256), 1) + 256 * w
+            whole = jnp.zeros((ROWS, 256), F32)
+            for k in range(6):
+                low = HEAD_DIM * (5 * w + k)
+                factor = inverse[5 * w + k]
+                piece = out[ROWS * k : ROWS * (k + 1)] * jnp.concatenate([factor, factor], axis=1)
+                whole = jnp.where(lane >= low, piece, whole)
+            att[:, lanes] = whole.astype(BF)
 
         for part in range(2):
             landed(kv.at[lp, part, own_rows], kv_send.at[lp, part])
@@ -440,6 +443,10 @@
     @pl.when(active)
     def _():
         conditions()
+
+        @pl.when(core == 1)
+        def _():
+            bias_on()
 
         @pl.when(s == 0)
         def _():
@@ -556,6 +563,10 @@
             pltpu.VMEM((ROWS, FF), BF),
             pltpu.VMEM((8, COND_PAD, D), BF),
             pltpu.VMEM((COND_PAD, D), BF),
+            pltpu.VMEM((6 * ROWS, 256), BF),
+            pltpu.VMEM((3, 6 * ROWS, KEYS), F32),
+            pltpu.VMEM((HEADS * ROWS, KEYS), BF),
+            pltpu.VMEM((HEADS, ROWS, 128), F32),
             dma((2,)), dma((TOK_DEVS,)),
             dma((POSES,)), dma((TOK_DEVS,)),
             dma((POSES,)), dma((TOK_DEVS,)),

time: 172 us -> 154 us (0.90)
  Pallas kernels: 169 us -> 151 us
    pallas_call x1, Pallas kernels: 169 us -> 151 us  [body(): pl.pallas_call(kernel, out_shape=jax.ShapeDtypeStruct((TOK_DEV, D), BF),...]
where the time goes in v3:
time: 154 us; the launch traced here: 153 us
  Pallas kernels  151 us (98%)
    pallas_call x1, Pallas kernels, body(): pl.pallas_call(kernel, out_shape=jax.ShapeDtypeStruct((TOK_DEV, D), BF),...  151 us

profile of v3, /device:TPU:17, one launch (start us, length us, event | category | flops | bytes accessed | tf_op | source)
XLA Modules:
  0.0 152.8 jit_solution(14883664099717921587)
XLA Ops:
  0.0 151.4 %shard_map.118 = bf16[24,768]{1,0:T(8,128)(2,1)} custom-call(f32[3,1,216]{2,1,0:T(1,128)} %bitcast.16, bf16[216,128]{1,0:T(8,128)(2,1)} %atom_ref.1, s32[1,24]{1,0:T(1,128)} %bitcast.17, bf16[24,768]{1,0:T(8,128)(2,1)} %cond_ref.1, bf16[384,384]{1,0:T(8,128)(2,1)} %bitcast.14, f32[3,128]{1,0:T(4,128)} %wcoord_ref.1, bf16[128,768]{1,0:T(8,128)(2,1)} %win_ref.1, ...), custom_call_target="tpu_custom_call" | custom-call | tf_op jit(solution)/shard_map/pallas_call | solution.py:534
  151.4 1.4 copy.14

commit v4 on v3

--- a/solution.py
+++ b/solution.py
@@ -18,7 +18,7 @@
 ATOM_PAD = 224
 COND_PAD = 32
 KEYS = 384
-GROUP = 384
+QUARTER = 96
 MESH = pl.DeviceIdType.MESH
 BF = jnp.bfloat16
 F32 = jnp.float32
@@ -72,17 +72,21 @@
     def greet(section, tok):
         pl.semaphore_signal(barrier, inc=1, device_id=(section, tok), device_id_type=MESH)
 
+    @pl.loop(1, TOK_DEVS)
+    def _(j):
+        greet(s, lax.rem(t + j, TOK_DEVS))
+
+    def beside(k):
+        step = 1 + 2 * lax.rem(k, 2)
+        return jnp.where(
+            k < 2, 4 * lax.rem(cx + step, 4) + cz, 4 * cx + lax.rem(cz + step, 4)
+        )
+
     @pl.when(active)
     def _():
-        @pl.loop(0, TOK_DEVS)
-        def _(j):
-            @pl.when(j != t)
-            def _():
-                greet(s, j)
-
-        @pl.loop(0, TOK_DEVS)
-        def _(j):
-            greet(sibling, j)
+        @pl.loop(0, 4)
+        def _(k):
+            greet(sibling, beside(k))
 
         @pl.when((s == 0) & (pose != 0))
         def _():
@@ -99,11 +103,6 @@
             greet(s - 2, t)
 
     greet(sibling, t)
-
-    @pl.loop(1, 4)
-    def _(k):
-        greet(s, 4 * lax.rem(cx + k, 4) + cz)
-        greet(s, 4 * cx + lax.rem(cz + k, 4))
 
     fin_section, fin_tok = 6 + half, chip_of(s)
     fin_self = (fin_section == s) & (fin_tok == t)
@@ -126,8 +125,7 @@
 
     one = lambda flag: flag.astype(jnp.int32)
     last = t == TOK_DEVS - 1
-    expected = 8 - one(active)
-    expected += 8 + 1 + 6
+    expected = 15 + 1 + 4 * (1 - one(active))
     expected += one(s != 0) + one(last & (s != 1))
     expected += one(active & (plane < 3))
     fin_here = active & (plane == 3)
@@ -170,62 +168,55 @@
     def _(p):
         send(d_src, d_all.at[t], d_send.at[p], d_recv.at[t], s, chip_of(p))
 
-    def legs(part, at, k):
-        if part == 0:
-            return 4 * lax.rem(cx + k, 4) + cz
-        return 4 * cx + lax.rem(cz + k, 4)
-
-    def half_of(part):
-        return bias_ref.at[pl.ds(ROWS * part, ROWS)]
-
-    def forward(part, at, source, act):
-        origin = 4 * at + cz if part == 0 else 4 * cx + at
-        block = lax.rem(origin, 8)
-        for e in range(2):
-            if part == 0:
-                tok = 4 * cx + lax.rem(cx, 2) + 2 * e
-            else:
-                tok = 4 * (lax.rem(cz, 2) + 2 * e) + cz
-            act(source, b_all.at[core, block, pl.ds(ROWS * part, ROWS)], b_send.at[part, at, e],
-                b_recv.at[core, block, part], 2 * plane + origin // 8, tok)
+    quarter = 2 * lax.rem(cx, 2) + lax.rem(cz + 2 * (cx // 2), 4) // 2
+
+    def bias_part(k):
+        return bias_ref.at[pl.ds(pl.multiple_of(QUARTER * k, QUARTER), QUARTER)]
+
+    def relay_chip(k, e):
+        first = k // 2
+        return 4 * (first + 2 * e) + lax.rem(2 * lax.rem(k, 2) + 1 - first + 2 * e, 4)
 
     def bias_out():
-        for part in range(2):
-            here = cx if part == 0 else cz
-
-            @pl.loop(1, 4)
+        @pl.loop(0, 8)
+        def _(j):
+            k, e = lax.rem(j, 4), j // 4
+            send(bias_part(k), relay.at[t], r_send.at[j], r_recv.at[t], s, relay_chip(k, e))
+
+    def bias_out_gone():
+        @pl.loop(0, 8)
+        def _(j):
+            k, e = lax.rem(j, 4), j // 4
+            sent(bias_part(k), r_send.at[j], s, relay_chip(k, e))
+
+    def bias_on():
+        @pl.loop(0, 4)
+        def _(g):
+            @pl.loop(0, 4)
+            def _(j):
+                landed(relay.at[4 * g + j], r_recv.at[4 * g + j])
+
+            @pl.loop(0, 4)
             def _(k):
                 pltpu.make_async_remote_copy(
-                    src_ref=half_of(part), dst_ref=relay.at[part, here],
-                    send_sem=r_send.at[part, k], recv_sem=r_recv.at[part, here],
-                    device_id=(s, legs(part, here, k)), device_id_type=MESH,
+                    src_ref=relay.at[pl.ds(4 * g, 4)],
+                    dst_ref=b_all.at[
+                        core, pl.ds(4 * lax.rem(g, 2), 4),
+                        pl.ds(pl.multiple_of(QUARTER * quarter, QUARTER), QUARTER),
+                    ],
+                    send_sem=b_send.at[g, k], recv_sem=b_recv.at[core, lax.rem(g, 2), quarter],
+                    device_id=(2 * plane + g // 2, beside(k)), device_id_type=MESH,
                 ).start()
 
-    def bias_on():
-        for part in range(2):
-            forward(part, cx if part == 0 else cz, half_of(part), send)
-
-        @pl.loop(1, 4)
-        def _(k):
-            for part in range(2):
-                at = lax.rem((cx if part == 0 else cz) + k, 4)
-                landed(relay.at[part, at], r_recv.at[part, at])
-                forward(part, at, relay.at[part, at], send)
-
     def bias_gone():
-        def gone(source, target, send_sem, recv_sem, section, tok):
-            sent(source, send_sem, section, tok)
-
-        for part in range(2):
+        @pl.loop(0, 4)
+        def _(g):
             @pl.loop(0, 4)
             def _(k):
-                at = lax.rem((cx if part == 0 else cz) + k, 4)
-
-                @pl.when(k > 0)
-                def _():
-                    landed(half_of(part), r_send.at[part, k])
-
-                forward(part, at, half_of(part), gone)
+                landed(relay.at[pl.ds(4 * g, 4)], b_send.at[g, k])
+
+    def tell():
+        pl.semaphore_signal(go, inc=1, device_id=(sibling, t), device_id_type=MESH)
 
     @pl.when(active)
     def _():
@@ -235,21 +226,25 @@
                 recv_sem=w_recv.at[core, k], device_id=(sibling, t), device_id_type=MESH,
             ).start()
 
-    bias_out()
-
     @pl.when(core == 0)
     def _():
+        bias_out()
+
+    @pl.when((core == 0) & jnp.logical_not(active))
+    def _():
+        bias_out_gone()
+        tell()
         bias_on()
-
-    @pl.when((core == 0) & jnp.logical_not(active))
-    def _():
         bias_gone()
-        pl.semaphore_signal(go, inc=1, device_id=(sibling, t), device_id_type=MESH)
+        tell()
 
     @pl.when((core == 1) & jnp.logical_not(active))
     def _():
+        pl.semaphore_wait(go, 1)
+        bias_out()
         pl.semaphore_wait(go, 1)
         bias_on()
+        bias_out_gone()
         bias_gone()
 
     def act_of(points, single):
@@ -282,15 +277,17 @@
         upper = jnp.concatenate([ends, ends], axis=1)[:, :ATOM_PAD]
         lane = lax.broadcasted_iota(jnp.int32, (ROWS, ATOM_PAD), 1)
 
-        def block(j, pooled):
+        @pl.loop(0, TOK_DEVS)
+        def _(j):
             landed(a_all.at[j], a_recv.at[j])
+
+        pooled = jnp.zeros((ROWS, 128), F32)
+        for j in range(TOK_DEVS):
             place = (lane + j * ATOM_DEV).astype(F32)
             inside = (place >= lower) & (place < upper) & (lane < ATOM_DEV)
             member = jnp.where(inside, 1.0, 0.0).astype(BF)
             act = act_of(c_all[j], a_all[j]).astype(BF)
-            return pooled + jnp.dot(member, act, preferred_element_type=F32)
-
-        pooled = lax.fori_loop(0, TOK_DEVS, block, jnp.zeros((ROWS, 128), F32))
+            pooled = pooled + jnp.dot(member, act, preferred_element_type=F32)
         averaged = (pooled / counts).astype(BF)
         x[...] = jnp.dot(averaged, win_ref[...], preferred_element_type=F32)
 
@@ -359,10 +356,13 @@
         for j in range(3):
             q[:, 256 * j : 256 * (j + 1)] = project(256 * j, 256)
 
-        @pl.loop(0, 16)
+        @pl.loop(0, 8)
         def _(j):
-            block = b_all.at[lp, j // 2, pl.ds(ROWS * lax.rem(j, 2), ROWS)]
-            landed(block, b_recv.at[lp, j // 2, lax.rem(j, 2)])
+            g, k = j // 4, lax.rem(j, 4)
+            block = b_all.at[
+                lp, pl.ds(4 * g, 4), pl.ds(pl.multiple_of(QUARTER * k, QUARTER), QUARTER)
+            ]
+            landed(block, b_recv.at[lp, g, k])
 
         for part in range(2):
             landed(kv.at[lp, part, other_rows], kv_recv.at[lp, part])
@@ -446,7 +446,7 @@
 
         @pl.when(core == 1)
         def _():
-            bias_on()
+            bias_out()
 
         @pl.when(s == 0)
         def _():
@@ -508,7 +508,7 @@
         for k, (src, dst) in enumerate(weights):
             landed(src, w_send.at[k])
         landed(cond_tx, m_send)
-        bias_gone()
+        bias_out_gone()
 
         @pl.when(plane < 3)
         def _():
@@ -545,7 +545,7 @@
             pltpu.VMEM((TOK_DEVS, ATOM_PAD, 128), BF),
             pltpu.VMEM((TOK_DEVS, COND_PAD, D), BF),
             pltpu.VMEM((2, 8, HEADS * TOK_DEV, KEYS), BF),
-            pltpu.VMEM((2, 4, ROWS, KEYS), BF),
+            pltpu.VMEM((TOK_DEVS, QUARTER, KEYS), BF),
             pltpu.VMEM((D, 4 * D), BF),
             pltpu.VMEM((2, D, 3 * D), BF),
             pltpu.VMEM((2, D, D), BF),
@@ -570,8 +570,8 @@
             dma((2,)), dma((TOK_DEVS,)),
             dma((POSES,)), dma((TOK_DEVS,)),
             dma((POSES,)), dma((TOK_DEVS,)),
-            dma((2, 4)), dma((2, 4)),
-            dma((2, 4, 2)), dma((2, 8, 2)),
+            dma((8,)), dma((TOK_DEVS,)),
+            dma((4, 4)), dma((2, 2, 4)),
             pltpu.SemaphoreType.REGULAR,
             dma((4,)), dma((2, 4)),
             dma,

time: 154 us -> 142 us (0.922)
  Pallas kernels: 151 us -> 138 us
    pallas_call x1, Pallas kernels: 151 us -> 138 us  [body(): pl.pallas_call(kernel, out_shape=jax.ShapeDtypeStruct((TOK_DEV, D), BF),...]
where the time goes in v4:
time: 142 us; the launch traced here: 140 us
  Pallas kernels  138 us (97%)
    pallas_call x1, Pallas kernels, body(): pl.pallas_call(kernel, out_shape=jax.ShapeDtypeStruct((TOK_DEV, D), BF),...  138 us

profile of v4, /device:TPU:17, one launch (start us, length us, event | category | flops | bytes accessed | tf_op | source)
XLA Modules:
  0.0 139.9 jit_solution(3929362101210621376)
XLA Ops:
  0.0 138.5 %shard_map.118 = bf16[24,768]{1,0:T(8,128)(2,1)} custom-call(f32[3,1,216]{2,1,0:T(1,128)} %bitcast.16, bf16[216,128]{1,0:T(8,128)(2,1)} %atom_ref.1, s32[1,24]{1,0:T(1,128)} %bitcast.17, bf16[24,768]{1,0:T(8,128)(2,1)} %cond_ref.1, bf16[384,384]{1,0:T(8,128)(2,1)} %bitcast.14, f32[3,128]{1,0:T(4,128)} %wcoord_ref.1, bf16[128,768]{1,0:T(8,128)(2,1)} %win_ref.1, ...), custom_call_target="tpu_custom_call" | custom-call | tf_op jit(solution)/shard_map/pallas_call | solution.py:534
  138.5 1.4 copy.14

commit v5 on v4

--- a/solution.py
+++ b/solution.py
@@ -47,7 +47,7 @@
     cond, cond_tx, x, xin, xtx, norm, q, kv, att, hid, fin_tx, fin,
     spread, scores, probs, inverse,
     c_send, c_recv, a_send, a_recv, d_send, d_recv, r_send, r_recv, b_send, b_recv, go,
-    w_send, w_recv, ada_sem, m_send, m_recv, kv_send, kv_recv, x_send, x_recv, f_send, f_recv,
+    w_send, w_recv, ada_sem, p_send, p_recv, m_send, m_recv, kv_send, kv_recv, x_send, x_recv, f_send, f_recv,
 ):
     s = lax.axis_index("section")
     t = lax.axis_index("tok")
@@ -119,9 +119,8 @@
     a_src[...] = jnp.concatenate(
         [atom_ref[...].astype(F32), jnp.zeros((ATOM_PAD - ATOM_DEV, 128), F32)], axis=0
     ).astype(BF)
-    d_src[...] = jnp.concatenate(
-        [cond_ref[...].astype(F32), jnp.zeros((COND_PAD - TOK_DEV, D), F32)], axis=0
-    ).astype(BF)
+    single = cond_ref[...].astype(F32)
+    d_src[...] = jnp.concatenate([single[:, :KEYS], single[:, KEYS:]], axis=0).astype(BF)
 
     one = lambda flag: flag.astype(jnp.int32)
     last = t == TOK_DEVS - 1
@@ -158,16 +157,6 @@
     def _():
         send(c_src, c_all.at[t], c_send.at[1], c_recv.at[t], 1, chip_of(s))
 
-    @pl.when((s == 0) | ((s == 1) & last))
-    def _():
-        @pl.loop(0, POSES)
-        def _(p):
-            send(a_src, a_all.at[t], a_send.at[p], a_recv.at[t], s, chip_of(p))
-
-    @pl.loop(0, POSES)
-    def _(p):
-        send(d_src, d_all.at[t], d_send.at[p], d_recv.at[t], s, chip_of(p))
-
     quarter = 2 * lax.rem(cx, 2) + lax.rem(cz + 2 * (cx // 2), 4) // 2
 
     def bias_part(k):
@@ -190,33 +179,48 @@
             sent(bias_part(k), r_send.at[j], s, relay_chip(k, e))
 
     def bias_on():
-        @pl.loop(0, 4)
-        def _(g):
-            @pl.loop(0, 4)
-            def _(j):
-                landed(relay.at[4 * g + j], r_recv.at[4 * g + j])
+        @pl.loop(0, TOK_DEVS)
+        def _(j):
+            origin = lax.rem(t + j, TOK_DEVS)
+            landed(relay.at[origin], r_recv.at[origin])
 
             @pl.loop(0, 4)
             def _(k):
                 pltpu.make_async_remote_copy(
-                    src_ref=relay.at[pl.ds(4 * g, 4)],
+                    src_ref=relay.at[origin],
                     dst_ref=b_all.at[
-                        core, pl.ds(4 * lax.rem(g, 2), 4),
+                        core, lax.rem(origin, 8),
                         pl.ds(pl.multiple_of(QUARTER * quarter, QUARTER), QUARTER),
                     ],
-                    send_sem=b_send.at[g, k], recv_sem=b_recv.at[core, lax.rem(g, 2), quarter],
-                    device_id=(2 * plane + g // 2, beside(k)), device_id_type=MESH,
+                    send_sem=b_send.at[j, k], recv_sem=b_recv.at[core],
+                    device_id=(2 * plane + origin // 8, beside(k)), device_id_type=MESH,
                 ).start()
 
-    def bias_gone():
-        @pl.loop(0, 4)
-        def _(g):
+    def bias_gone(low, high):
+        @pl.loop(low, high)
+        def _(j):
             @pl.loop(0, 4)
             def _(k):
-                landed(relay.at[pl.ds(4 * g, 4)], b_send.at[g, k])
+                landed(relay.at[0], b_send.at[j, k])
 
     def tell():
         pl.semaphore_signal(go, inc=1, device_id=(sibling, t), device_id_type=MESH)
+
+    @pl.when(core == 0)
+    def _():
+        bias_out()
+
+    @pl.when((s == 0) | ((s == 1) & last))
+    def _():
+        @pl.loop(0, POSES)
+        def _(p):
+            send(a_src, a_all.at[t], a_send.at[p], a_recv.at[t], s, chip_of(p))
+
+    @pl.when(core == 1)
+    def _():
+        @pl.loop(0, POSES)
+        def _(p):
+            send(d_src, d_all.at[t], d_send.at[p], d_recv.at[t], s, chip_of(p))
 
     @pl.when(active)
     def _():
@@ -228,24 +232,27 @@
 
     @pl.when(core == 0)
     def _():
-        bias_out()
-
-    @pl.when((core == 0) & jnp.logical_not(active))
-    def _():
         bias_out_gone()
         tell()
-        bias_on()
-        bias_gone()
-        tell()
-
-    @pl.when((core == 1) & jnp.logical_not(active))
+
+    @pl.when(core == 1)
     def _():
         pl.semaphore_wait(go, 1)
         bias_out()
+
+    @pl.when((core == 0) & jnp.logical_not(active))
+    def _():
+        bias_on()
+        bias_gone(0, 12)
+        tell()
+        bias_gone(12, 16)
+
+    @pl.when((core == 1) & jnp.logical_not(active))
+    def _():
         pl.semaphore_wait(go, 1)
         bias_on()
         bias_out_gone()
-        bias_gone()
+        bias_gone(0, 16)
 
     def act_of(points, single):
         moved = lax.dot_general(
@@ -299,19 +306,33 @@
         x[...] = jnp.dot(act.astype(BF), win_ref[...], preferred_element_type=F32)
 
     def conditions():
-        @pl.loop(0, TOK_DEVS)
-        def _(j):
-            landed(d_all.at[j], d_recv.at[j])
+        @pl.when(core == 1)
+        def _():
+            @pl.loop(0, TOK_DEVS)
+            def _(j):
+                landed(d_all.at[j], d_recv.at[j])
+
+            pltpu.make_async_remote_copy(
+                src_ref=d_all, dst_ref=d_all, send_sem=p_send, recv_sem=p_recv,
+                device_id=(sibling, t), device_id_type=MESH,
+            ).start()
+
+        @pl.when(core == 0)
+        def _():
+            landed(d_all, p_recv)
 
         landed(wada_ref, ada_sem)
 
         def rows_for(which, store):
-            rows = d_all[pl.ds(8 * which, 8)].reshape(8 * COND_PAD, D)
+            blocks = d_all[pl.ds(8 * which, 8)].astype(F32)
+            norm[...] = jnp.concatenate(
+                [blocks[:, :TOK_DEV].reshape(ROWS, KEYS), blocks[:, TOK_DEV:].reshape(ROWS, KEYS)],
+                axis=1,
+            ).astype(BF)
             for k in range(4):
-                full = jnp.dot(
-                    rows, wada_v[:, D * k : D * (k + 1)], preferred_element_type=F32
+                value = jnp.dot(
+                    norm[...], wada_v[:, D * k : D * (k + 1)], preferred_element_type=F32
                 )
-                value = full.reshape(8, COND_PAD, D)[:, :TOK_DEV].reshape(ROWS, D)
                 store(k, jax.nn.sigmoid(value) if k % 2 == 0 else value)
 
         def to_send(k, value):
@@ -343,66 +364,51 @@
                 norm[...], wqkv_v[lp, :, column : column + width], preferred_element_type=F32
             ).astype(BF)
 
+        def tile(part, j, rows):
+            return kv.at[lp, part, j, rows]
+
         for part in range(2):
             for j in range(3):
-                kv[lp, part, own_rows, 256 * j : 256 * (j + 1)] = project(
-                    D * (part + 1) + 256 * j, 256
-                )
+                kv[lp, part, j, own_rows, :] = project(D * (part + 1) + 256 * j, 256)
             pltpu.make_async_remote_copy(
-                src_ref=kv.at[lp, part, own_rows], dst_ref=kv.at[lp, part, own_rows],
-                send_sem=kv_send.at[lp, part], recv_sem=kv_recv.at[lp, part],
+                src_ref=kv.at[lp, part, :, own_rows], dst_ref=kv.at[lp, part, :, own_rows],
+                send_sem=kv_send.at[lp, part, 0], recv_sem=kv_recv.at[lp, part, 0],
                 device_id=(sibling, t), device_id_type=MESH,
             ).start()
         for j in range(3):
             q[:, 256 * j : 256 * (j + 1)] = project(256 * j, 256)
 
-        @pl.loop(0, 8)
-        def _(j):
-            g, k = j // 4, lax.rem(j, 4)
-            block = b_all.at[
-                lp, pl.ds(4 * g, 4), pl.ds(pl.multiple_of(QUARTER * k, QUARTER), QUARTER)
-            ]
-            landed(block, b_recv.at[lp, g, k])
-
-        for part in range(2):
-            landed(kv.at[lp, part, other_rows], kv_recv.at[lp, part])
-
-        for w in range(3):
-            lanes = slice(256 * w, 256 * (w + 1))
-            window = q[:, lanes]
+        def score(w):
+            window = q[:, 256 * w : 256 * (w + 1)]
             lane = lax.broadcasted_iota(jnp.int32, (1, 256), 1) + 256 * w
             for k in range(6):
                 low = HEAD_DIM * (5 * w + k)
                 mask = jnp.where((lane >= low) & (lane < low + HEAD_DIM), 1.0, 0.0).astype(BF)
-                spread[ROWS * k : ROWS * (k + 1)] = window * mask
+                spread[w, ROWS * k : ROWS * (k + 1)] = window * mask
             scores[w] = lax.dot_general(
-                spread[...], kv[lp, 0, :, lanes], (((1,), (1,)), ((), ())),
-                preferred_element_type=F32,
+                spread[w], kv[lp, 0, w], (((1,), (1,)), ((), ())), preferred_element_type=F32
             )
 
-        for pair in range(8):
+        def soften(head):
+            pair, e = head // 2, head % 2
             bias = b_all[lp, :, 48 * pair : 48 * (pair + 1), :].astype(F32)
-            for e in range(2):
-                head = 2 * pair + e
-                w = min(head // 5, 2)
-                k = head - 5 * w
-                raw = scores[w, ROWS * k : ROWS * (k + 1)]
-                if k == 0 and w > 0:
-                    raw = raw + scores[w - 1, 5 * ROWS : 6 * ROWS]
-                logits = raw * HEAD_DIM ** (-0.5) + bias[
-                    :, TOK_DEV * e : TOK_DEV * (e + 1)
-                ].reshape(ROWS, KEYS)
-                top = jnp.max(logits, axis=-1, keepdims=True)
-                weight = jnp.exp(logits - top)
-                total = jnp.sum(weight, axis=-1, keepdims=True)
-                inverse[head] = jnp.broadcast_to(1.0 / total, (ROWS, 128))
-                probs[ROWS * head : ROWS * (head + 1)] = weight.astype(BF)
-
-        for w in range(3):
-            lanes = slice(256 * w, 256 * (w + 1))
+            w = min(head // 5, 2)
+            k = head - 5 * w
+            raw = scores[w, ROWS * k : ROWS * (k + 1)]
+            if k == 0 and w > 0:
+                raw = raw + scores[w - 1, 5 * ROWS : 6 * ROWS]
+            logits = raw * HEAD_DIM ** (-0.5) + bias[
+                :, TOK_DEV * e : TOK_DEV * (e + 1)
+            ].reshape(ROWS, KEYS)
+            top = jnp.max(logits, axis=-1, keepdims=True)
+            weight = jnp.exp(logits - top)
+            total = jnp.sum(weight, axis=-1, keepdims=True)
+            inverse[head] = jnp.broadcast_to(1.0 / total, (ROWS, 128))
+            probs[ROWS * head : ROWS * (head + 1)] = weight.astype(BF)
+
+        def gather(w):
             out = jnp.dot(
-                probs[ROWS * 5 * w : ROWS * (5 * w + 6)], kv[lp, 1, :, lanes],
-                preferred_element_type=F32,
+                probs[ROWS * 5 * w : ROWS * (5 * w + 6)], kv[lp, 1, w], preferred_element_type=F32
             )
             lane = lax.broadcasted_iota(jnp.int32, (1, 256), 1) + 256 * w
             whole = jnp.zeros((ROWS, 256), F32)
@@ -411,10 +417,27 @@
                 factor = inverse[5 * w + k]
                 piece = out[ROWS * k : ROWS * (k + 1)] * jnp.concatenate([factor, factor], axis=1)
                 whole = jnp.where(lane >= low, piece, whole)
-            att[:, lanes] = whole.astype(BF)
+            att[:, 256 * w : 256 * (w + 1)] = whole.astype(BF)
+
+        landed(kv.at[lp, 0, :, other_rows], kv_recv.at[lp, 0, 0])
+        score(0)
+        score(1)
+        score(2)
+        landed(kv.at[lp, 1, :, other_rows], kv_recv.at[lp, 1, 0])
+
+        landed(b_all.at[lp], b_recv.at[lp])
+        for head in range(0, 6):
+            soften(head)
+        gather(0)
+        for head in range(6, 11):
+            soften(head)
+        gather(1)
+        for head in range(11, 16):
+            soften(head)
+        gather(2)
 
         for part in range(2):
-            landed(kv.at[lp, part, own_rows], kv_send.at[lp, part])
+            landed(kv.at[lp, part, :, own_rows], kv_send.at[lp, part, 0])
 
         landed(wout_v.at[lp], w_recv.at[lp, 1])
         for j in range(3):
@@ -444,10 +467,6 @@
     def _():
         conditions()
 
-        @pl.when(core == 1)
-        def _():
-            bias_out()
-
         @pl.when(s == 0)
         def _():
             enter_first()
@@ -499,16 +518,23 @@
         def _(p):
             sent(a_src, a_send.at[p], s, chip_of(p))
 
-    @pl.loop(0, POSES)
-    def _(p):
-        sent(d_src, d_send.at[p], s, chip_of(p))
+    @pl.when(core == 1)
+    def _():
+        @pl.loop(0, POSES)
+        def _(p):
+            sent(d_src, d_send.at[p], s, chip_of(p))
 
     @pl.when(active)
     def _():
         for k, (src, dst) in enumerate(weights):
             landed(src, w_send.at[k])
         landed(cond_tx, m_send)
-        bias_out_gone()
+
+        @pl.when(core == 1)
+        def _():
+            landed(d_all, p_send)
+            bias_out_gone()
+
 
         @pl.when(plane < 3)
         def _():
@@ -539,11 +565,11 @@
         scratch_shapes=[
             pltpu.VMEM((8, 256), F32),
             pltpu.VMEM((ATOM_PAD, 128), BF),
-            pltpu.VMEM((COND_PAD, D), BF),
+            pltpu.VMEM((2 * TOK_DEV, KEYS), BF),
             pltpu.VMEM((8, 128), F32),
             pltpu.VMEM((TOK_DEVS, 8, 256), F32),
             pltpu.VMEM((TOK_DEVS, ATOM_PAD, 128), BF),
-            pltpu.VMEM((TOK_DEVS, COND_PAD, D), BF),
+            pltpu.VMEM((TOK_DEVS, 2 * TOK_DEV, KEYS), BF),
             pltpu.VMEM((2, 8, HEADS * TOK_DEV, KEYS), BF),
             pltpu.VMEM((TOK_DEVS, QUARTER, KEYS), BF),
             pltpu.VMEM((D, 4 * D), BF),
@@ -558,12 +584,12 @@
             pltpu.VMEM((ROWS, D), BF),
             pltpu.VMEM((ROWS, D), BF),
             pltpu.VMEM((ROWS, D), BF),
-            pltpu.VMEM((2, 2, KEYS, D), BF),
+            pltpu.VMEM((2, 2, 3, KEYS, 256), BF),
             pltpu.VMEM((ROWS, D), BF),
             pltpu.VMEM((ROWS, FF), BF),
             pltpu.VMEM((8, COND_PAD, D), BF),
             pltpu.VMEM((COND_PAD, D), BF),
-            pltpu.VMEM((6 * ROWS, 256), BF),
+            pltpu.VMEM((3, 6 * ROWS, 256), BF),
             pltpu.VMEM((3, 6 * ROWS, KEYS), F32),
             pltpu.VMEM((HEADS * ROWS, KEYS), BF),
             pltpu.VMEM((HEADS, ROWS, 128), F32),
@@ -571,12 +597,13 @@
             dma((POSES,)), dma((TOK_DEVS,)),
             dma((POSES,)), dma((TOK_DEVS,)),
             dma((8,)), dma((TOK_DEVS,)),
-            dma((4, 4)), dma((2, 2, 4)),
+            dma((TOK_DEVS, 4)), dma((2,)),
             pltpu.SemaphoreType.REGULAR,
             dma((4,)), dma((2, 4)),
             dma,
             dma, dma,
-            dma((2, 2)), dma((2, 2)),
+            dma, dma,
+            dma((2, 2, 3)), dma((2, 2, 3)),
             dma, dma,
             dma((8,)), dma,
         ],

time: 142 us -> 138 us (0.972)
  Pallas kernels: 138 us -> 134 us
    pallas_call x1, Pallas kernels: 138 us -> 134 us  [body(): pl.pallas_call(kernel, out_shape=jax.ShapeDtypeStruct((TOK_DEV, D), BF),...]
where the time goes in v5:
time: 138 us; the launch traced here: 136 us
  Pallas kernels  134 us (97%)
  local copies, waits for them, and re-layouts  1.39 us (1%)
    pallas_call x1, Pallas kernels, body(): pl.pallas_call(kernel, out_shape=jax.ShapeDtypeStruct((TOK_DEV, D), BF),...  134 us

profile of v5, /device:TPU:17, one launch (start us, length us, event | category | flops | bytes accessed | tf_op | source)
XLA Modules:
  0.0 135.5 jit_solution(12509559490865474647)
XLA Ops:
  0.0 134.1 %shard_map.118 = bf16[24,768]{1,0:T(8,128)(2,1)} custom-call(f32[3,1,216]{2,1,0:T(1,128)} %bitcast.16, bf16[216,128]{1,0:T(8,128)(2,1)} %atom_ref.1, s32[1,24]{1,0:T(1,128)} %bitcast.17, bf16[24,768]{1,0:T(8,128)(2,1)} %cond_ref.1, bf16[384,384]{1,0:T(8,128)(2,1)} %bitcast.14, f32[3,128]{1,0:T(4,128)} %wcoord_ref.1, bf16[128,768]{1,0:T(8,128)(2,1)} %win_ref.1, ...), custom_call_target="tpu_custom_call" | custom-call | tf_op jit(solution)/shard_map/pallas_call | solution.py:560
  134.1 1.4 %copy.14 = bf16[1,24,768]{2,1,0:T(8,128)(2,1)} copy(bf16[1,24,768]{2,1,0:T(8,128)(2,1)} %bitcast.15) | data formatting | bytes 73728

commit v6 on v5

--- a/solution.py
+++ b/solution.py
@@ -39,11 +39,12 @@
 
 
 def kernel(
-    coords_ref, atom_ref, count_ref, cond_ref, bias_ref, wcoord_ref, win_ref,
+    coords_in, atom_ref, count_in, cond_ref, bias_in, wcoord_in, win_in,
     wada_ref, wqkv_ref, wout_ref, wff_ref, wdown_ref,
     out_ref,
+    coords_ref, count_ref, wcoord_ref, win_ref, fetch,
     c_src, a_src, d_src, wc, c_all, a_all, d_all, b_all, relay,
-    wada_v, wqkv_v, wout_v, wff_v, wdown_v,
+    wada_v, wqkv_v, wout_v, wff_v, wdown_v, bias_v, bias_t,
     cond, cond_tx, x, xin, xtx, norm, q, kv, att, hid, fin_tx, fin,
     spread, scores, probs, inverse,
     c_send, c_recv, a_send, a_recv, d_send, d_recv, r_send, r_recv, b_send, b_recv, go,
@@ -59,6 +60,13 @@
     pose = 2 * cx + cz // 2
     half = t // 8
 
+    fetched = (
+        (coords_in, coords_ref), (count_in, count_ref),
+        (wcoord_in, wcoord_ref), (win_in, win_ref), (bias_in, bias_v),
+    )
+    for k, (src, dst) in enumerate(fetched):
+        pltpu.make_async_copy(src, dst, fetch.at[k]).start()
+
     weights = ((wqkv_ref, wqkv_v), (wout_ref, wout_v), (wff_ref, wff_v), (wdown_ref, wdown_v))
 
     @pl.when(active)
@@ -110,6 +118,18 @@
     @pl.when(jnp.logical_not(fin_self))
     def _():
         greet(fin_section, fin_tok)
+
+    for k, (src, dst) in enumerate(fetched):
+        pltpu.make_async_copy(src, dst, fetch.at[k]).wait()
+
+    @pl.when(half == 0)
+    def _():
+        bias_t[...] = bias_v[...]
+
+    @pl.when(half == 1)
+    def _():
+        straight = bias_v[...].astype(F32)
+        bias_t[...] = jnp.concatenate([straight[:, ROWS:], straight[:, :ROWS]], axis=1).astype(BF)
 
     c_src[...] = jnp.zeros_like(c_src)
     c_src[0:3, 0:ATOM_DEV] = coords_ref[...].reshape(3, ATOM_DEV)
@@ -160,7 +180,7 @@
     quarter = 2 * lax.rem(cx, 2) + lax.rem(cz + 2 * (cx // 2), 4) // 2
 
     def bias_part(k):
-        return bias_ref.at[pl.ds(pl.multiple_of(QUARTER * k, QUARTER), QUARTER)]
+        return bias_t.at[pl.ds(pl.multiple_of(QUARTER * k, QUARTER), QUARTER)]
 
     def relay_chip(k, e):
         first = k // 2
@@ -179,21 +199,22 @@
             sent(bias_part(k), r_send.at[j], s, relay_chip(k, e))
 
     def bias_on():
-        @pl.loop(0, TOK_DEVS)
+        @pl.loop(0, 8)
         def _(j):
-            origin = lax.rem(t + j, TOK_DEVS)
-            landed(relay.at[origin], r_recv.at[origin])
+            pair = lax.rem(t // 2 + j, 8)
+            for e in range(2):
+                landed(relay.at[2 * pair + e], r_recv.at[2 * pair + e])
 
             @pl.loop(0, 4)
             def _(k):
                 pltpu.make_async_remote_copy(
-                    src_ref=relay.at[origin],
+                    src_ref=relay.at[pl.ds(2 * pair, 2)],
                     dst_ref=b_all.at[
-                        core, lax.rem(origin, 8),
+                        core, pl.ds(2 * lax.rem(pair, 4), 2),
                         pl.ds(pl.multiple_of(QUARTER * quarter, QUARTER), QUARTER),
                     ],
                     send_sem=b_send.at[j, k], recv_sem=b_recv.at[core],
-                    device_id=(2 * plane + origin // 8, beside(k)), device_id_type=MESH,
+                    device_id=(2 * plane + pair // 4, beside(k)), device_id_type=MESH,
                 ).start()
 
     def bias_gone(low, high):
@@ -201,7 +222,7 @@
         def _(j):
             @pl.loop(0, 4)
             def _(k):
-                landed(relay.at[0], b_send.at[j, k])
+                landed(relay.at[pl.ds(0, 2)], b_send.at[j, k])
 
     def tell():
         pl.semaphore_signal(go, inc=1, device_id=(sibling, t), device_id_type=MESH)
@@ -243,16 +264,16 @@
     @pl.when((core == 0) & jnp.logical_not(active))
     def _():
         bias_on()
-        bias_gone(0, 12)
+        bias_gone(0, 6)
         tell()
-        bias_gone(12, 16)
+        bias_gone(6, 8)
 
     @pl.when((core == 1) & jnp.logical_not(active))
     def _():
         pl.semaphore_wait(go, 1)
         bias_on()
         bias_out_gone()
-        bias_gone(0, 16)
+        bias_gone(0, 8)
 
     def act_of(points, single):
         moved = lax.dot_general(
@@ -348,45 +369,39 @@
         ).start()
         rows_for(core, to_keep)
 
-    own_rows = pl.ds(pl.multiple_of(core * ROWS, ROWS), ROWS)
-    other_rows = pl.ds(pl.multiple_of((1 - core) * ROWS, ROWS), ROWS)
+    mine, theirs = slice(0, ROWS), slice(ROWS, KEYS)
 
     def layer(lp):
-        @pl.when(lp != core)
-        def _():
-            landed(cond.at[lp], m_recv)
-
         norm[...] = (normalise(x[...]) * cond[lp, 0] + cond[lp, 1]).astype(BF)
-        landed(wqkv_v.at[lp], w_recv.at[lp, 0])
 
         def project(column, width):
             return jnp.dot(
                 norm[...], wqkv_v[lp, :, column : column + width], preferred_element_type=F32
             ).astype(BF)
 
-        def tile(part, j, rows):
-            return kv.at[lp, part, j, rows]
-
         for part in range(2):
             for j in range(3):
-                kv[lp, part, j, own_rows, :] = project(D * (part + 1) + 256 * j, 256)
+                kv[lp, part, j, mine, :] = project(D * (part + 1) + 256 * j, 256)
             pltpu.make_async_remote_copy(
-                src_ref=kv.at[lp, part, :, own_rows], dst_ref=kv.at[lp, part, :, own_rows],
-                send_sem=kv_send.at[lp, part, 0], recv_sem=kv_recv.at[lp, part, 0],
+                src_ref=kv.at[lp, part, :, mine], dst_ref=kv.at[lp, part, :, theirs],
+                send_sem=kv_send.at[lp, part], recv_sem=kv_recv.at[lp, part],
                 device_id=(sibling, t), device_id_type=MESH,
             ).start()
         for j in range(3):
             q[:, 256 * j : 256 * (j + 1)] = project(256 * j, 256)
 
-        def score(w):
+        def spread_out(w):
             window = q[:, 256 * w : 256 * (w + 1)]
             lane = lax.broadcasted_iota(jnp.int32, (1, 256), 1) + 256 * w
             for k in range(6):
                 low = HEAD_DIM * (5 * w + k)
                 mask = jnp.where((lane >= low) & (lane < low + HEAD_DIM), 1.0, 0.0).astype(BF)
                 spread[w, ROWS * k : ROWS * (k + 1)] = window * mask
-            scores[w] = lax.dot_general(
-                spread[w], kv[lp, 0, w], (((1,), (1,)), ((), ())), preferred_element_type=F32
+
+        def score(w, first, stop):
+            scores[w, :, first:stop] = lax.dot_general(
+                spread[w], kv[lp, 0, w, first:stop], (((1,), (1,)), ((), ())),
+                preferred_element_type=F32,
             )
 
         def soften(head):
@@ -419,12 +434,13 @@
                 whole = jnp.where(lane >= low, piece, whole)
             att[:, 256 * w : 256 * (w + 1)] = whole.astype(BF)
 
-        landed(kv.at[lp, 0, :, other_rows], kv_recv.at[lp, 0, 0])
-        score(0)
-        score(1)
-        score(2)
-        landed(kv.at[lp, 1, :, other_rows], kv_recv.at[lp, 1, 0])
-
+        for w in range(3):
+            spread_out(w)
+            score(w, 0, 128)
+        landed(kv.at[lp, 0, :, theirs], kv_recv.at[lp, 0])
+        for w in range(3):
+            score(w, 128, KEYS)
+        landed(kv.at[lp, 1, :, theirs], kv_recv.at[lp, 1])
         landed(b_all.at[lp], b_recv.at[lp])
         for head in range(0, 6):
             soften(head)
@@ -436,17 +452,12 @@
             soften(head)
         gather(2)
 
-        for part in range(2):
-            landed(kv.at[lp, part, :, own_rows], kv_send.at[lp, part, 0])
-
-        landed(wout_v.at[lp], w_recv.at[lp, 1])
         for j in range(3):
             cols = slice(256 * j, 256 * (j + 1))
             x[:, cols] = x[:, cols] + jnp.dot(
                 att[...], wout_v[lp, :, cols], preferred_element_type=F32
             )
         norm[...] = (normalise(x[...]) * cond[lp, 2] + cond[lp, 3]).astype(BF)
-        landed(wff_v.at[lp], w_recv.at[lp, 2])
         for j in range(6):
             gate = jnp.dot(
                 norm[...], wff_v[lp, :, 256 * j : 256 * (j + 1)], preferred_element_type=F32
@@ -456,7 +467,6 @@
                 preferred_element_type=F32,
             )
             hid[:, 256 * j : 256 * (j + 1)] = (jax.nn.silu(gate) * up).astype(BF)
-        landed(wdown_v.at[lp], w_recv.at[lp, 3])
         for j in range(3):
             cols = slice(256 * j, 256 * (j + 1))
             x[:, cols] = x[:, cols] + jnp.dot(
@@ -475,6 +485,11 @@
         def _():
             enter_second()
 
+        for k, (src, dst) in enumerate(weights):
+            for lp in range(2):
+                landed(dst.at[lp], w_recv.at[lp, k])
+        landed(cond.at[1 - core], m_recv)
+
         @pl.when(plane > 0)
         def _():
             landed(xin, x_recv)
@@ -529,6 +544,11 @@
         for k, (src, dst) in enumerate(weights):
             landed(src, w_send.at[k])
         landed(cond_tx, m_send)
+
+        @pl.loop(0, 2)
+        def _(lp):
+            for part in range(2):
+                landed(kv.at[lp, part, :, mine], kv_send.at[lp, part])
 
         @pl.when(core == 1)
         def _():
@@ -560,9 +580,14 @@
     rows = pl.pallas_call(
         kernel,
         out_shape=jax.ShapeDtypeStruct((TOK_DEV, D), BF),
-        in_specs=[vmem, vmem, vmem, vmem, hbm, vmem, vmem, hbm, hbm, hbm, hbm, hbm],
+        in_specs=[hbm, vmem, hbm, vmem] + [hbm] * 8,
         out_specs=vmem,
         scratch_shapes=[
+            pltpu.VMEM((3, 1, ATOM_DEV), F32),
+            pltpu.VMEM((1, TOK_DEV), jnp.int32),
+            pltpu.VMEM((3, 128), F32),
+            pltpu.VMEM((128, D), BF),
+            dma((5,)),
             pltpu.VMEM((8, 256), F32),
             pltpu.VMEM((ATOM_PAD, 128), BF),
             pltpu.VMEM((2 * TOK_DEV, KEYS), BF),
@@ -577,6 +602,8 @@
             pltpu.VMEM((2, D, D), BF),
             pltpu.VMEM((2, D, 2 * FF), BF),
             pltpu.VMEM((2, FF, D), BF),
+            pltpu.VMEM((HEADS * TOK_DEV, KEYS), BF),
+            pltpu.VMEM((HEADS * TOK_DEV, KEYS), BF),
             pltpu.VMEM((2, 4, ROWS, D), F32),
             pltpu.VMEM((4, ROWS, D), F32),
             pltpu.VMEM((ROWS, D), F32),
@@ -597,13 +624,13 @@
             dma((POSES,)), dma((TOK_DEVS,)),
             dma((POSES,)), dma((TOK_DEVS,)),
             dma((8,)), dma((TOK_DEVS,)),
-            dma((TOK_DEVS, 4)), dma((2,)),
+            dma((8, 4)), dma((2,)),
             pltpu.SemaphoreType.REGULAR,
             dma((4,)), dma((2, 4)),
             dma,
             dma, dma,
             dma, dma,
-            dma((2, 2, 3)), dma((2, 2, 3)),
+            dma((2, 2)), dma((2, 2)),
             dma, dma,
             dma((8,)), dma,
         ],

time: 138 us -> 132 us (0.957); the launches traced: 136 us -> 132 us
  Pallas kernels: 134 us -> 130 us
    pallas_call x1, Pallas kernels: 134 us -> 130 us  [body(): pl.pallas_call(kernel, out_shape=jax.ShapeDtypeStruct((TOK_DEV, D), BF),...]
where the time goes in v6:
time: 132 us
  Pallas kernels  130 us (98%)
  local copies, waits for them, and re-layouts  1.39 us (1%)
    pallas_call x1, Pallas kernels, body(): pl.pallas_call(kernel, out_shape=jax.ShapeDtypeStruct((TOK_DEV, D), BF),...  130 us

profile of v6, /device:TPU:17, one launch (start us, length us, event | category | flops | bytes accessed | tf_op | source)
XLA Modules:
  0.0 131.8 jit_solution(6707718273246499829)
XLA Ops:
  0.0 130.4 %shard_map.118 = bf16[24,768]{1,0:T(8,128)(2,1)} custom-call(f32[3,1,216]{2,1,0:T(1,128)} %bitcast.16, bf16[216,128]{1,0:T(8,128)(2,1)} %atom_ref.1, s32[1,24]{1,0:T(1,128)} %bitcast.17, bf16[24,768]{1,0:T(8,128)(2,1)} %cond_ref.1, bf16[384,384]{1,0:T(8,128)(2,1)} %bitcast.14, f32[3,128]{1,0:T(4,128)} %wcoord_in.1, bf16[128,768]{1,0:T(8,128)(2,1)} %win_in.1, ...), custom_call_target="tpu_custom_call" | custom-call | tf_op jit(solution)/shard_map/pallas_call | solution.py:580
  130.4 1.4 %copy.14 = bf16[1,24,768]{2,1,0:T(8,128)(2,1)} copy(bf16[1,24,768]{2,1,0:T(8,128)(2,1)} %bitcast.15) | data formatting | bytes 73728

commit v7 on v6

--- a/solution.py
+++ b/solution.py
@@ -438,10 +438,10 @@
             spread_out(w)
             score(w, 0, 128)
         landed(kv.at[lp, 0, :, theirs], kv_recv.at[lp, 0])
+        landed(kv.at[lp, 1, :, theirs], kv_recv.at[lp, 1])
+        landed(b_all.at[lp], b_recv.at[lp])
         for w in range(3):
             score(w, 128, KEYS)
-        landed(kv.at[lp, 1, :, theirs], kv_recv.at[lp, 1])
-        landed(b_all.at[lp], b_recv.at[lp])
         for head in range(0, 6):
             soften(head)
         gather(0)

time: 132 us -> 127 us (0.962)
  Pallas kernels: 130 us -> 125 us
    pallas_call x1, Pallas kernels: 130 us -> 125 us  [body(): pl.pallas_call(kernel, out_shape=jax.ShapeDtypeStruct((TOK_DEV, D), BF),...]
where the time goes in v7:
time: 127 us; the launch traced here: 126 us
  Pallas kernels  125 us (98%)
  local copies, waits for them, and re-layouts  1.39 us (1%)
    pallas_call x1, Pallas kernels, body(): pl.pallas_call(kernel, out_shape=jax.ShapeDtypeStruct((TOK_DEV, D), BF),...  125 us

profile of v7, /device:TPU:17, one launch (start us, length us, event | category | flops | bytes accessed | tf_op | source)
XLA Modules:
  0.0 126.4 jit_solution(10280246978399331151)
XLA Ops:
  0.0 125.0 %shard_map.118 = bf16[24,768]{1,0:T(8,128)(2,1)} custom-call(f32[3,1,216]{2,1,0:T(1,128)} %bitcast.16, bf16[216,128]{1,0:T(8,128)(2,1)} %atom_ref.1, s32[1,24]{1,0:T(1,128)} %bitcast.17, bf16[24,768]{1,0:T(8,128)(2,1)} %cond_ref.1, bf16[384,384]{1,0:T(8,128)(2,1)} %bitcast.14, f32[3,128]{1,0:T(4,128)} %wcoord_in.1, bf16[128,768]{1,0:T(8,128)(2,1)} %win_in.1, ...), custom_call_target="tpu_custom_call" | custom-call | tf_op jit(solution)/shard_map/pallas_call | solution.py:580
  125.0 1.4 %copy.14 = bf16[1,24,768]{2,1,0:T(8,128)(2,1)} copy(bf16[1,24,768]{2,1,0:T(8,128)(2,1)} %bitcast.15) | data formatting | bytes 73728

commit v8 on v7

--- a/solution.py
+++ b/solution.py
@@ -382,11 +382,11 @@
         for part in range(2):
             for j in range(3):
                 kv[lp, part, j, mine, :] = project(D * (part + 1) + 256 * j, 256)
-            pltpu.make_async_remote_copy(
-                src_ref=kv.at[lp, part, :, mine], dst_ref=kv.at[lp, part, :, theirs],
-                send_sem=kv_send.at[lp, part], recv_sem=kv_recv.at[lp, part],
-                device_id=(sibling, t), device_id_type=MESH,
-            ).start()
+        pltpu.make_async_remote_copy(
+            src_ref=kv.at[lp, :, :, mine], dst_ref=kv.at[lp, :, :, theirs],
+            send_sem=kv_send.at[lp], recv_sem=kv_recv.at[lp],
+            device_id=(sibling, t), device_id_type=MESH,
+        ).start()
         for j in range(3):
             q[:, 256 * j : 256 * (j + 1)] = project(256 * j, 256)
 
@@ -437,8 +437,7 @@
         for w in range(3):
             spread_out(w)
             score(w, 0, 128)
-        landed(kv.at[lp, 0, :, theirs], kv_recv.at[lp, 0])
-        landed(kv.at[lp, 1, :, theirs], kv_recv.at[lp, 1])
+        landed(kv.at[lp, :, :, theirs], kv_recv.at[lp])
         landed(b_all.at[lp], b_recv.at[lp])
         for w in range(3):
             score(w, 128, KEYS)
@@ -469,9 +468,11 @@
             hid[:, 256 * j : 256 * (j + 1)] = (jax.nn.silu(gate) * up).astype(BF)
         for j in range(3):
             cols = slice(256 * j, 256 * (j + 1))
-            x[:, cols] = x[:, cols] + jnp.dot(
+            state = x[:, cols] + jnp.dot(
                 hid[...], wdown_v[lp, :, cols], preferred_element_type=F32
             )
+            x[:, cols] = state
+            xtx[:, cols] = state.astype(BF)
 
     @pl.when(active)
     def _():
@@ -501,7 +502,6 @@
 
         @pl.when(plane < 3)
         def _():
-            xtx[...] = x[...].astype(BF)
             pltpu.make_async_remote_copy(
                 src_ref=xtx, dst_ref=xin, send_sem=x_send, recv_sem=x_recv,
                 device_id=(s + 2, t), device_id_type=MESH,
@@ -547,8 +547,7 @@
 
         @pl.loop(0, 2)
         def _(lp):
-            for part in range(2):
-                landed(kv.at[lp, part, :, mine], kv_send.at[lp, part])
+            landed(kv.at[lp, :, :, mine], kv_send.at[lp])
 
         @pl.when(core == 1)
         def _():
@@ -630,7 +629,7 @@
             dma,
             dma, dma,
             dma, dma,
-            dma((2, 2)), dma((2, 2)),
+            dma((2,)), dma((2,)),
             dma, dma,
             dma((8,)), dma,
         ],

time: 127 us -> 127 us (level)
  no operation moved by 1% of the time
where the time goes in v8:
time: 127 us
  Pallas kernels  125 us (98%)
  local copies, waits for them, and re-layouts  1.39 us (1%)
    pallas_call x1, Pallas kernels, body(): pl.pallas_call(kernel, out_shape=jax.ShapeDtypeStruct((TOK_DEV, D), BF),...  125 us

profile of v8, /device:TPU:17, one launch (start us, length us, event | category | flops | bytes accessed | tf_op | source)
XLA Modules:
  0.0 126.8 jit_solution(10017042183604658103)
XLA Ops:
  0.0 125.4 %shard_map.118 = bf16[24,768]{1,0:T(8,128)(2,1)} custom-call(f32[3,1,216]{2,1,0:T(1,128)} %bitcast.16, bf16[216,128]{1,0:T(8,128)(2,1)} %atom_ref.1, s32[1,24]{1,0:T(1,128)} %bitcast.17, bf16[24,768]{1,0:T(8,128)(2,1)} %cond_ref.1, bf16[384,384]{1,0:T(8,128)(2,1)} %bitcast.14, f32[3,128]{1,0:T(4,128)} %wcoord_in.1, bf16[128,768]{1,0:T(8,128)(2,1)} %win_in.1, ...), custom_call_target="tpu_custom_call" | custom-call | tf_op jit(solution)/shard_map/pallas_call | solution.py:579
  125.4 1.4 %copy.14 = bf16[1,24,768]{2,1,0:T(8,128)(2,1)} copy(bf16[1,24,768]{2,1,0:T(8,128)(2,1)} %bitcast.15) | data formatting | bytes 73728
